TPU v7x, 32 devices: a whole 2x2x4 slice. The times are simulated.
32 devices in a mesh: band: 8 (over z, x), slab: 4 (over y, core).
Axes of the slice: x: 2, y: 2, z: 4, core: 2. Of those that a mesh axis runs over, the one named last changes fastest.
Arguments:
- orbitals: float32 [16, 128, 128, 128], P('band', 'slab'), may hold values from -6 to 6
- slot_ids: int32 [16], P('band'), may hold values from 0 to 15, each once
- occupations: float32 [16], replicated, may hold values from 0.25 to 2
- mode_lists: int32 [3, 48], replicated, may hold values from 0 to 127, as said below
Outputs:
- exchange_terms: float32 [16, 128, 128, 128], P('band', 'slab')
Inputs may be any that keep to these rules, and one draw needn't show every extreme that they name: `slot_ids`: each number appears once. `mode_lists`: each row lists 48 different mode numbers, among them 0 and 127.
All inputs are finite; a program needn't handle non-finite values.
Results may differ from a plain program's by a relative error of at most 0.000059.
Values sent between devices are 32-bit elements; how exact they have to be, the bound alone decides.
A program may use at most 128 MiB of HBM per device.

v0:
```python
import jax
import jax.numpy as jnp
from jax import lax
from jax.sharding import PartitionSpec as P


def passed_along(value, axis, steps):
    count = lax.axis_size(axis)
    pairs = [(source, (source + steps) % count) for source in range(count)]
    return lax.ppermute(value, axis, pairs)


def sine_table(mode_row, points):
    grid = jnp.arange(points, dtype=jnp.int32) + 1
    phase = grid[:, None] * (mode_row[None, :] + 1) % (2 * points + 2)
    angle = jnp.pi * phase.astype(jnp.float32) / (points + 1.0)
    return jnp.sqrt(jnp.float32(2.0) / (points + 1.0)) * jnp.sin(angle)


def screen_table(first, second, third, points):
    squares = (
        ((first + 1) ** 2)[:, None, None]
        + ((second + 1) ** 2)[None, :, None]
        + ((third + 1) ** 2)[None, None, :]
    )
    return 1.0 / (1.0 + squares.astype(jnp.float32) / jnp.float32(points * points))


def on_device(orbitals, slot_ids, occupations, mode_lists):
    highest = lax.Precision.HIGHEST
    planes = orbitals.shape[1]
    points = orbitals.shape[2]
    count = mode_lists.shape[1]
    groups = lax.axis_size("slab")
    share = count // groups
    width = share * count
    sine_first = sine_table(mode_lists[0], points)
    sine_second = sine_table(mode_lists[1], points)
    sine_third = sine_table(mode_lists[2], points)
    local_modes = lax.dynamic_slice_in_dim(mode_lists[1], lax.axis_index("slab") * share, share)
    screen_local = screen_table(mode_lists[0], local_modes, mode_lists[2], points).reshape(
        count, width
    )
    catalog = jnp.arange(occupations.shape[0], dtype=jnp.int32)
    own_weight = jnp.sum(
        jnp.where(slot_ids[:, None] == catalog[None, :], occupations[None, :], 0.0), axis=1
    )
    own_scaled = own_weight[:, None, None, None] * orbitals

    def modal(block):
        items = block.shape[0]
        flat = block.reshape(items, points, width)
        spectral = (
            jnp.einsum("nxc,xa->nac", flat, sine_first, precision=highest) * screen_local[None]
        )
        spatial = jnp.einsum("nac,xa->nxc", spectral, sine_first, precision=highest)
        spatial = spatial.reshape(items, points, 1, width)
        return lax.all_to_all(spatial, "slab", split_axis=1, concat_axis=2, tiled=True)

    def pair_solve(left, right):
        lead = left.shape[0]
        other = right.shape[0]
        pairs = lead * other
        density = (left[:, None] * right[None, :]).reshape(pairs * planes * points, points)
        coeffs = jnp.dot(density, sine_third, precision=highest).reshape(
            pairs, planes, points, count
        )
        coeffs = jnp.einsum("nxyk,yj->nxjk", coeffs, sine_second, precision=highest)
        coeffs = coeffs.reshape(pairs, planes, groups, width)
        returned = modal(lax.all_to_all(coeffs, "slab", split_axis=2, concat_axis=1, tiled=True))
        returned = returned.reshape(pairs, planes, count, count)
        field = jnp.einsum("nxjk,yj->nxyk", returned, sine_second, precision=highest)
        field = jnp.dot(
            field.reshape(pairs * planes * points, count), sine_third.T, precision=highest
        )
        return field.reshape(lead, other, planes, points, points)

    def gathered(field, visitors, visit_weight):
        return jnp.sum(field * (visit_weight[:, None, None, None] * visitors)[None], axis=1)

    field = pair_solve(orbitals, orbitals)
    totals = jnp.sum(field * own_scaled[None], axis=1)
    bands = lax.axis_size("band")
    half = bands // 2
    visitors, visit_weight = passed_along((orbitals, own_weight), "band", 1)
    field = pair_solve(orbitals, visitors)
    totals = totals + gathered(field, visitors, visit_weight)
    carried = jnp.sum(field * own_scaled[:, None], axis=0)

    def carry_step(step_index, carry):
        running, visitors, visit_weight, partial_terms = carry
        visitors, visit_weight, partial_terms = passed_along(
            (visitors, visit_weight, partial_terms), "band", 1
        )
        solved = pair_solve(orbitals, visitors)
        running = running + gathered(solved, visitors, visit_weight)
        partial_terms = partial_terms + jnp.sum(solved * own_scaled[:, None], axis=0)
        return (running, visitors, visit_weight, partial_terms)

    totals, visitors, visit_weight, carried = lax.fori_loop(
        2, half, carry_step, (totals, visitors, visit_weight, carried)
    )
    home_terms = passed_along(carried, "band", 1 - half)
    visitors, visit_weight = passed_along((visitors, visit_weight), "band", 1)
    field = pair_solve(orbitals, visitors)
    totals = totals + gathered(field, visitors, visit_weight) + home_terms
    return totals


def solution(mesh):
    in_specs = (P("band", "slab", None, None), P("band"), P(), P())
    out_specs = P("band", "slab", None, None)
    return jax.shard_map(
        on_device, mesh=mesh, in_specs=in_specs, out_specs=out_specs, check_vma=False
    )
```

profile of v0, /device:TPU:0, one launch (start us, length us, event | category | flops | bytes accessed | tf_op | source)
XLA Modules:
  0.0 1044.0 jit_solution(13137740403449306619)
XLA Ops:
  3.7 93.1 %collective-permute-done.3 = f32[2,32,128,128]{3,2,1,0:T(8,128)} collective-permute-done((f32[2,32,128,128]{3,2,1,0:T(8,128)}, f32[2,32,128,128]{3,2,1,0:T(8,128)}, u32[]{:S(2)}, u32[]{:S(2)}) %collective-permute-start.3) | collective-permute-done | bytes 4194336 | tf_op jit(solution)/shard_map/ppermute | solution.py:10
  96.9 7.7 broadcast_multiply_fusion.3
  104.6 9.4 fusion.129
  114.0 11.1 %convolution_bitcast_fusion.4 = f32[4,32,48,48]{3,2,1,0:T(8,128)S(1)} fusion(f32[4,32,128,48]{2,3,1,0:T(8,128)S(1)} %fusion.129, s32[48]{0:T(128)S(1)} %get-tuple-element.274, s32[128]{0:T(128)S(1)} %iota_add_fusion), kind=kOutput, calls=%fused_computation.119 | convolution fusion | flops 453046272 | bytes 4326080 | tf_op jit(solution)/shard_map/nxyk,yj->nxjk/dot_general | solution.py:68
  134.2 11.8 %fusion.131 = f32[4,32,128,48]{2,3,1,0:T(8,128)S(1)} fusion(f32[4,32,128,128]{3,2,1,0:T(8,128)} %bitcast.237, s32[48]{0:T(128)S(1)} %get-tuple-element.272, s32[128]{0:T(128)S(1)} %iota_add_fusion), kind=kOutput, calls=%fused_computation.157 | convolution fusion | flops 1208020992 | bytes 11535040 | tf_op jit(solution)/shard_map/dot_general | solution.py:65
  146.0 10.9 %convolution_bitcast_fusion.5 = f32[4,32,48,48]{3,2,1,0:T(8,128)S(1)} fusion(f32[4,32,128,48]{2,3,1,0:T(8,128)S(1)} %fusion.131, s32[48]{0:T(128)S(1)} %get-tuple-element.274, s32[128]{0:T(128)S(1)} %iota_add_fusion), kind=kOutput, calls=%fused_computation.120 | convolution fusion | flops 453046272 | bytes 4326080 | tf_op jit(solution)/shard_map/nxyk,yj->nxjk/dot_general | solution.py:68
  172.3 10.5 %all-to-all-done.2 = f32[4,32,4,576]{3,1,0,2:T(8,128)S(1)} async-done(((f32[4,32,4,576]{3,1,0,2:T(8,128)}), f32[4,32,4,576]{3,1,0,2:T(8,128)S(1)}, u32[]{:S(2)}, u32[]{:S(2)}) %all-to-all-start.2) | async-done | bytes 1179680 | tf_op jit(solution)/shard_map/all_to_all | solution.py:70
  191.3 12.2 %all-to-all-done.5 = f32[4,128,1,576]{3,0,2,1:T(4,128)S(1)} async-done(((f32[4,128,1,576]{3,0,2,1:T(4,128)}), f32[4,128,1,576]{3,0,2,1:T(4,128)S(1)}, u32[]{:S(2)}, u32[]{:S(2)}) %all-to-all-start.5) | async-done | bytes 1179680 | tf_op jit(solution)/shard_map/all_to_all | solution.py:58
  222.0 7.0 fusion.143
  236.9 7.3 fusion.146
  244.3 14.5 %multiply_reduce_fusion.5 = f32[2,32,128,128]{3,2,1,0:T(8,128)S(1)} fusion(f32[2,32,128,128]{3,2,1,0:T(8,128)S(1)} %copy-done.3, f32[2,2,32,128,48]{3,4,2,1,0:T(8,128)S(1)} %bitcast.242, s32[48]{0:T(128)S(1)} %get-tuple-element.272, s32[128]{0:T(128)S(1)} %iota_add_fusion), kind=kOutput, calls=%fused_computation.110 | convolution fusion | flops 1211166720 | bytes 11535040 | tf_op jit(solution)/shard_map/dot_general | solution.py:73
  258.8 17.9 %multiply_reduce_fusion.3 = (f32[2,32,128,128]{3,2,1,0:T(8,128)}, f32[2,32,128,128]{3,2,1,0:T(8,128)S(1)}) fusion(f32[2,32,128,128]{3,2,1,0:T(8,128)S(1)} %copy-done.3, f32[2,32,128,128]{3,2,1,0:T(8,128)S(1)} %copy-done.7, f32[2,2,32,128,48]{3,4,2,1,0:T(8,128)S(1)} %bitcast.240, s32[48]{0:T(128)S(1)} %get-tuple-element.272, s32[128]{0:T(128)S(1)} %iota_add_fusion), kind=kOutput, calls=%fused_computation.108 | convolution fusion | flops 1214312448 | bytes 19923648 | tf_op jit(solution)/shard_map/dot_general | solution.py:73
  279.4 488.4 %while.18 = (s32[]{:T(128)}, f32[2,32,128,128]{3,2,1,0:T(8,128)}, f32[2,32,128,128]{3,2,1,0:T(8,128)}, f32[2]{0:T(128)S(1)}, f32[2,32,128,128]{3,2,1,0:T(8,128)}...) while((s32[]{:T(128)}, f32[2,32,128,128]{3,2,1,0:T(8,128)}, ...), condition=%wide.region_7.8_spmd.clone.clone, body=%wide.region_4.7_spmd.clone.clone.sunk | while | flops 3673779200 | bytes 246439008 | solution.py:100
  302.9 95.1 %collective-permute-done = f32[2,32,128,128]{3,2,1,0:T(8,128)S(1)} collective-permute-done((f32[2,32,128,128]{3,2,1,0:T(8,128)}, f32[2,32,128,128]{3,2,1,0:T(8,128)S(1)}, u32[]{:S(2)}, u32[]{:S(2)}) %collective-permute-start) | collective-permute-done | bytes 4194336 | tf_op jit(solution)/shard_map/while/body/eval_jaxpr/ppermute | solution.py:10
  403.0 9.5 fusion.359
  427.8 16.9 %all-to-all-done = f32[4,32,4,576]{3,1,0,2:T(8,128)S(1)} async-done(((f32[4,32,4,576]{3,1,0,2:T(8,128)}), f32[4,32,4,576]{3,1,0,2:T(8,128)S(1)}, u32[]{:S(2)}, u32[]{:S(2)}) %all-to-all-start) | async-done | bytes 1179680 | tf_op jit(solution)/shard_map/while/body/eval_jaxpr/all_to_all | solution.py:70
  453.1 34.5 %collective-permute-done.1 = f32[2]{0:T(128)S(1)} collective-permute-done((f32[2]{0:T(128)S(1)}, f32[2]{0:T(128)S(1)}, u32[]{:S(2)}, u32[]{:S(2)}) %collective-permute-start.1) | collective-permute-done | bytes 40 | tf_op jit(solution)/shard_map/while/body/eval_jaxpr/ppermute | solution.py:10
  505.4 17.6 %multiply_reduce_fusion.7 = (f32[2,32,128,128]{3,2,1,0:T(8,128)S(1)}, f32[2,32,128,128]{3,2,1,0:T(8,128)S(1)}) fusion(f32[2,32,128,128]{3,2,1,0:T(8,128)} %get-tuple-element.299, f32[2,32,128,128]{3,2,1,0:T(8,128)S(1)} %copy-done, f32[2,2,32,128,48]{3,4,2,1,0:T(8,128)S(1)} %bitcast.233, s32[48]{0:T(128)S(1)} %get-tuple-element.300, ...), kind=kOutput, calls=%fused_computation.4.clone.1 | convolution fusion | flops 1214312448 | bytes 19923648 | tf_op jit(solution)/shard_map/while/body/eval_jaxpr/dot_general | solution.py:73
  524.4 6.4 add.353
  530.9 96.4 %collective-permute-done = f32[2,32,128,128]{3,2,1,0:T(8,128)S(1)} collective-permute-done((f32[2,32,128,128]{3,2,1,0:T(8,128)}, f32[2,32,128,128]{3,2,1,0:T(8,128)S(1)}, u32[]{:S(2)}, u32[]{:S(2)}) %collective-permute-start) | collective-permute-done | bytes 4194336 | tf_op jit(solution)/shard_map/while/body/eval_jaxpr/ppermute | solution.py:10
  632.2 9.4 fusion.359
  657.0 16.9 %all-to-all-done = f32[4,32,4,576]{3,1,0,2:T(8,128)S(1)} async-done(((f32[4,32,4,576]{3,1,0,2:T(8,128)}), f32[4,32,4,576]{3,1,0,2:T(8,128)S(1)}, u32[]{:S(2)}, u32[]{:S(2)}) %all-to-all-start) | async-done | bytes 1179680 | tf_op jit(solution)/shard_map/while/body/eval_jaxpr/all_to_all | solution.py:70
  682.3 33.6 %collective-permute-done.1 = f32[2]{0:T(128)S(1)} collective-permute-done((f32[2]{0:T(128)S(1)}, f32[2]{0:T(128)S(1)}, u32[]{:S(2)}, u32[]{:S(2)}) %collective-permute-start.1) | collective-permute-done | bytes 40 | tf_op jit(solution)/shard_map/while/body/eval_jaxpr/ppermute | solution.py:10
  733.7 17.6 %multiply_reduce_fusion.7 = (f32[2,32,128,128]{3,2,1,0:T(8,128)S(1)}, f32[2,32,128,128]{3,2,1,0:T(8,128)S(1)}) fusion(f32[2,32,128,128]{3,2,1,0:T(8,128)} %get-tuple-element.299, f32[2,32,128,128]{3,2,1,0:T(8,128)S(1)} %copy-done, f32[2,2,32,128,48]{3,4,2,1,0:T(8,128)S(1)} %bitcast.233, s32[48]{0:T(128)S(1)} %get-tuple-element.300, ...), kind=kOutput, calls=%fused_computation.4.clone.1 | convolution fusion | flops 1214312448 | bytes 19923648 | tf_op jit(solution)/shard_map/while/body/eval_jaxpr/dot_general | solution.py:73
  752.8 6.4 add.353
  767.9 96.3 %collective-permute-done.5 = f32[2,32,128,128]{3,2,1,0:T(8,128)S(1)} collective-permute-done((f32[2,32,128,128]{3,2,1,0:T(8,128)}, f32[2,32,128,128]{3,2,1,0:T(8,128)S(1)}, u32[]{:S(2)}, u32[]{:S(2)}) %collective-permute-start.5) | collective-permute-done | bytes 4194336 | tf_op jit(solution)/shard_map/ppermute | solution.py:10
  869.2 9.4 fusion.127
  878.7 11.1 %convolution_bitcast_fusion.3 = f32[4,32,48,48]{3,2,1,0:T(8,128)S(1)} fusion(f32[4,32,128,48]{2,3,1,0:T(8,128)S(1)} %fusion.127, s32[48]{0:T(128)S(1)} %get-tuple-element.323, s32[128]{0:T(128)S(1)} %get-tuple-element.320), kind=kOutput, calls=%fused_computation.118 | convolution fusion | flops 453046272 | bytes 4326080 | tf_op jit(solution)/shard_map/nxyk,yj->nxjk/dot_general | solution.py:68
  893.3 19.8 %all_to_all.130 = f32[4,32,4,576]{3,1,0,2:T(8,128)S(1)} all-to-all(f32[4,32,4,576]{3,1,0,2:T(8,128)S(1)} %copy.73), channel_id=1, replica_groups=mesh['band'=8,'slab'=4] {'slab'}, dimensions={2} | all-to-all | bytes 2359296 | tf_op jit(solution)/shard_map/all_to_all | solution.py:70
  921.5 85.2 %collective-permute-start.6 = (f32[2]{0:T(128)S(1)}, f32[2]{0:T(128)S(1)}, u32[]{:S(2)}, u32[]{:S(2)}) collective-permute-start(f32[2]{0:T(128)S(1)} %get-tuple-element.67), channel_id=1, source_target_pairs={{0,4},{4,8},{8,12},{12,16},{16,20},{20,24},{24,28},{28,0},{1,5},{5... | collective-permute-start | bytes 32 | tf_op jit(solution)/shard_map/ppermute | solution.py:10
  1023.5 14.7 %multiply_reduce_fusion.2 = f32[2,32,128,128]{3,2,1,0:T(8,128)S(1)} fusion(f32[2,32,128,128]{3,2,1,0:T(8,128)S(1)} %copy-done.8, f32[2,2,32,128,48]{3,4,2,1,0:T(8,128)S(1)} %bitcast.241, s32[48]{0:T(128)S(1)} %get-tuple-element.321, s32[128]{0:T(128)S(1)} %get-tuple-element.320), kind=kOutput, calls=%fused_computation.107 | convolution fusion | flops 1211166720 | bytes 11535040 | tf_op jit(solution)/shard_map/dot_general | solution.py:73
  1038.2 5.6 add_add_fusion
  (148 shorter events, 195.8 us)
Async XLA Ops:
  0.0 96.9 %collective-permute-start.3 = (f32[2,32,128,128]{3,2,1,0:T(8,128)}, f32[2,32,128,128]{3,2,1,0:T(8,128)}, u32[]{:S(2)}, u32[]{:S(2)}) collective-permute-start(f32[2,32,128,128]{3,2,1,0:T(8,128)} %param.6), channel_id=1, source_target_pairs={{0,4},{4,8},{8,12},{12,16},{16,20},{20,24},{24,28},{28,0},{1,5},{5... | collective-permute-start | bytes 12582920 | tf_op jit(solution)/shard_map/ppermute | solution.py:10
  129.8 31.7 %all-to-all-start.4 = ((f32[4,32,4,576]{3,1,0,2:T(8,128)}), f32[4,32,4,576]{3,1,0,2:T(8,128)}, u32[]{:S(2)}, u32[]{:S(2)}) async-start(f32[4,32,4,576]{3,1,0,2:T(8,128)} %copy.66), calls=%async_computation.4 | async-start | bytes 2621440 | tf_op jit(solution)/shard_map/all_to_all | solution.py:70
  161.6 21.2 %all-to-all-start.2 = ((f32[4,32,4,576]{3,1,0,2:T(8,128)}), f32[4,32,4,576]{3,1,0,2:T(8,128)S(1)}, u32[]{:S(2)}, u32[]{:S(2)}) async-start(f32[4,32,4,576]{3,1,0,2:T(8,128)} %copy.59), calls=%async_computation.2 | async-start | bytes 2621440 | tf_op jit(solution)/shard_map/all_to_all | solution.py:70
  166.2 20.5 %copy-start.10 = (f32[48,576]{1,0:T(8,128)}, f32[48,576]{1,0:T(8,128)S(1)}, u32[]{:S(2)}) copy-start(f32[48,576]{1,0:T(8,128)S(1)} %add_divide_fusion.1) | copy-start | bytes 331780
  168.6 17.7 %copy-start.12 = (f32[16]{0:T(128)S(1)}, f32[16]{0:T(128)}, u32[]{:S(2)}) copy-start(f32[16]{0:T(128)} %param.8) | copy-start | bytes 196
  168.7 17.7 %copy-start.13 = (s32[2]{0:T(128)S(1)}, s32[2]{0:T(128)}, u32[]{:S(2)}) copy-start(s32[2]{0:T(128)} %param.7) | copy-start | bytes 28
  182.8 20.8 %all-to-all-start.5 = ((f32[4,128,1,576]{3,0,2,1:T(4,128)}), f32[4,128,1,576]{3,0,2,1:T(4,128)S(1)}, u32[]{:S(2)}, u32[]{:S(2)}) async-start(f32[4,128,1,576]{3,0,2,1:T(4,128)} %copy.69), calls=%async_computation.5 | async-start | bytes 2621440 | tf_op jit(solution)/shard_map/all_to_all | solution.py:58
  186.5 26.4 %collective-permute-start.4 = (f32[2]{0:T(128)S(1)}, f32[2]{0:T(128)S(1)}, u32[]{:S(2)}, u32[]{:S(2)}) collective-permute-start(f32[2]{0:T(128)S(1)} %fusion.235), channel_id=1, source_target_pairs={{0,4},{4,8},{8,12},{12,16},{16,20},{20,24},{24,28},{28,0},{1,5},{5... | collective-permute-start | bytes 32 | tf_op jit(solution)/shard_map/ppermute | solution.py:10
  203.6 25.4 %all-to-all-start.3 = ((f32[4,128,1,576]{3,0,2,1:T(4,128)}), f32[4,128,1,576]{3,0,2,1:T(4,128)}, u32[]{:S(2)}, u32[]{:S(2)}) async-start(f32[4,128,1,576]{3,0,2,1:T(4,128)} %copy.62), calls=%async_computation.3 | async-start | bytes 2621440 | tf_op jit(solution)/shard_map/all_to_all | solution.py:58
  236.9 7.4 copy-start.3
  244.3 14.5 %copy-start.7 = (f32[2,32,128,128]{3,2,1,0:T(8,128)S(1)}, f32[2,32,128,128]{3,2,1,0:T(8,128)}, u32[]{:S(2)}) copy-start(f32[2,32,128,128]{3,2,1,0:T(8,128)} %broadcast_multiply_fusion.6) | copy-start | bytes 12582916
  301.7 96.3 %collective-permute-start = (f32[2,32,128,128]{3,2,1,0:T(8,128)}, f32[2,32,128,128]{3,2,1,0:T(8,128)S(1)}, u32[]{:S(2)}, u32[]{:S(2)}) collective-permute-start(f32[2,32,128,128]{3,2,1,0:T(8,128)} %get-tuple-element.281), channel_id=1, source_target_pairs={{0,4},{4,8},{8,12},{12,16},{16,20},{20,24},{24,28},{28,0},{1,5},{5... | collective-permute-start | bytes 12582920 | tf_op jit(solution)/shard_map/while/body/eval_jaxpr/ppermute | solution.py:10
  301.7 222.7 %collective-permute-start.2 = (f32[2,32,128,128]{3,2,1,0:T(8,128)}, f32[2,32,128,128]{3,2,1,0:T(8,128)}, u32[]{:S(2)}, u32[]{:S(2)}) collective-permute-start(f32[2,32,128,128]{3,2,1,0:T(8,128)} %get-tuple-element.283), channel_id=1, source_target_pairs={{0,4},{4,8},{8,12},{12,16},{16,20},{20,24},{24,28},{28,0},{1,5},{5... | collective-permute-start | bytes 12582920 | tf_op jit(solution)/shard_map/while/body/eval_jaxpr/ppermute | solution.py:10
  423.9 20.8 %all-to-all-start = ((f32[4,32,4,576]{3,1,0,2:T(8,128)}), f32[4,32,4,576]{3,1,0,2:T(8,128)S(1)}, u32[]{:S(2)}, u32[]{:S(2)}) async-start(f32[4,32,4,576]{3,1,0,2:T(8,128)} %copy.101), calls=%async_computation | async-start | bytes 2621440 | tf_op jit(solution)/shard_map/while/body/eval_jaxpr/all_to_all | solution.py:70
  449.5 45.4 %all-to-all-start.1 = ((f32[4,128,1,576]{3,0,2,1:T(4,128)}), f32[4,128,1,576]{3,0,2,1:T(4,128)S(1)}, u32[]{:S(2)}, u32[]{:S(2)}) async-start(f32[4,128,1,576]{3,0,2,1:T(4,128)} %copy.103), calls=%async_computation.1 | async-start | bytes 2621440 | tf_op jit(solution)/shard_map/while/body/eval_jaxpr/all_to_all | solution.py:58
  453.0 34.6 %collective-permute-start.1 = (f32[2]{0:T(128)S(1)}, f32[2]{0:T(128)S(1)}, u32[]{:S(2)}, u32[]{:S(2)}) collective-permute-start(f32[2]{0:T(128)S(1)} %get-tuple-element.282), channel_id=1, source_target_pairs={{0,4},{4,8},{8,12},{12,16},{16,20},{20,24},{24,28},{28,0},{1,5},{5... | collective-permute-start | bytes 32 | tf_op jit(solution)/shard_map/while/body/eval_jaxpr/ppermute | solution.py:10
  505.4 17.7 %copy-start.4 = (f32[2,32,128,128]{3,2,1,0:T(8,128)S(1)}, f32[2,32,128,128]{3,2,1,0:T(8,128)}, u32[]{:S(2)}) copy-start(f32[2,32,128,128]{3,2,1,0:T(8,128)} %get-tuple-element.280) | copy-start | bytes 12582916 | tf_op jit(solution)/shard_map/while
  524.4 6.4 copy-start.5
  530.8 96.4 %collective-permute-start = (f32[2,32,128,128]{3,2,1,0:T(8,128)}, f32[2,32,128,128]{3,2,1,0:T(8,128)S(1)}, u32[]{:S(2)}, u32[]{:S(2)}) collective-permute-start(f32[2,32,128,128]{3,2,1,0:T(8,128)} %get-tuple-element.281), channel_id=1, source_target_pairs={{0,4},{4,8},{8,12},{12,16},{16,20},{20,24},{24,28},{28,0},{1,5},{5... | collective-permute-start | bytes 12582920 | tf_op jit(solution)/shard_map/while/body/eval_jaxpr/ppermute | solution.py:10
  530.8 221.9 %collective-permute-start.2 = (f32[2,32,128,128]{3,2,1,0:T(8,128)}, f32[2,32,128,128]{3,2,1,0:T(8,128)}, u32[]{:S(2)}, u32[]{:S(2)}) collective-permute-start(f32[2,32,128,128]{3,2,1,0:T(8,128)} %get-tuple-element.283), channel_id=1, source_target_pairs={{0,4},{4,8},{8,12},{12,16},{16,20},{20,24},{24,28},{28,0},{1,5},{5... | collective-permute-start | bytes 12582920 | tf_op jit(solution)/shard_map/while/body/eval_jaxpr/ppermute | solution.py:10
  653.1 20.8 %all-to-all-start = ((f32[4,32,4,576]{3,1,0,2:T(8,128)}), f32[4,32,4,576]{3,1,0,2:T(8,128)S(1)}, u32[]{:S(2)}, u32[]{:S(2)}) async-start(f32[4,32,4,576]{3,1,0,2:T(8,128)} %copy.101), calls=%async_computation | async-start | bytes 2621440 | tf_op jit(solution)/shard_map/while/body/eval_jaxpr/all_to_all | solution.py:70
  678.7 44.5 %all-to-all-start.1 = ((f32[4,128,1,576]{3,0,2,1:T(4,128)}), f32[4,128,1,576]{3,0,2,1:T(4,128)S(1)}, u32[]{:S(2)}, u32[]{:S(2)}) async-start(f32[4,128,1,576]{3,0,2,1:T(4,128)} %copy.103), calls=%async_computation.1 | async-start | bytes 2621440 | tf_op jit(solution)/shard_map/while/body/eval_jaxpr/all_to_all | solution.py:58
  682.2 33.7 %collective-permute-start.1 = (f32[2]{0:T(128)S(1)}, f32[2]{0:T(128)S(1)}, u32[]{:S(2)}, u32[]{:S(2)}) collective-permute-start(f32[2]{0:T(128)S(1)} %get-tuple-element.282), channel_id=1, source_target_pairs={{0,4},{4,8},{8,12},{12,16},{16,20},{20,24},{24,28},{28,0},{1,5},{5... | collective-permute-start | bytes 32 | tf_op jit(solution)/shard_map/while/body/eval_jaxpr/ppermute | solution.py:10
  733.7 17.7 %copy-start.4 = (f32[2,32,128,128]{3,2,1,0:T(8,128)S(1)}, f32[2,32,128,128]{3,2,1,0:T(8,128)}, u32[]{:S(2)}) copy-start(f32[2,32,128,128]{3,2,1,0:T(8,128)} %get-tuple-element.280) | copy-start | bytes 12582916 | tf_op jit(solution)/shard_map/while
  752.7 6.4 copy-start.5
  767.8 96.5 %collective-permute-start.5 = (f32[2,32,128,128]{3,2,1,0:T(8,128)}, f32[2,32,128,128]{3,2,1,0:T(8,128)S(1)}, u32[]{:S(2)}, u32[]{:S(2)}) collective-permute-start(f32[2,32,128,128]{3,2,1,0:T(8,128)} %get-tuple-element.66), channel_id=1, source_target_pairs={{0,4},{4,8},{8,12},{12,16},{16,20},{20,24},{24,28},{28,0},{1,5},{5... | collective-permute-start | bytes 12582920 | tf_op jit(solution)/shard_map/ppermute | solution.py:10
  767.8 270.4 %collective-permute-start.7 = (f32[2,32,128,128]{3,2,1,0:T(8,128)}, f32[2,32,128,128]{3,2,1,0:T(8,128)}, u32[]{:S(2)}, u32[]{:S(2)}) collective-permute-start(f32[2,32,128,128]{3,2,1,0:T(8,128)} %get-tuple-element.68), channel_id=1, source_target_pairs={{0,20},{4,24},{8,28},{12,0},{16,4},{20,8},{24,12},{28,16},{1,21},{... | collective-permute-start | bytes 12582920 | tf_op jit(solution)/shard_map/ppermute | solution.py:10
  893.3 20.0 %copy-start.11 = (f32[48,576]{1,0:T(8,128)S(1)}, f32[48,576]{1,0:T(8,128)}, u32[]{:S(2)}) copy-start(f32[48,576]{1,0:T(8,128)} %copy-done.10) | copy-start | bytes 331780
  917.9 95.0 %all-to-all-start.7 = ((f32[4,128,1,576]{3,0,2,1:T(4,128)}), f32[4,128,1,576]{3,0,2,1:T(4,128)S(1)}, u32[]{:S(2)}, u32[]{:S(2)}) async-start(f32[4,128,1,576]{3,0,2,1:T(4,128)} %copy.76), calls=%async_computation.7 | async-start | bytes 2621440 | tf_op jit(solution)/shard_map/all_to_all | solution.py:58
  921.5 86.5 %collective-permute-start.6 = (f32[2]{0:T(128)S(1)}, f32[2]{0:T(128)S(1)}, u32[]{:S(2)}, u32[]{:S(2)}) collective-permute-start(f32[2]{0:T(128)S(1)} %get-tuple-element.67), channel_id=1, source_target_pairs={{0,4},{4,8},{8,12},{12,16},{16,20},{20,24},{24,28},{28,0},{1,5},{5... | collective-permute-start | bytes 32 | tf_op jit(solution)/shard_map/ppermute | solution.py:10
  1018.2 5.3 copy-start.8
  1023.5 14.7 %copy-start.6 = (f32[2,32,128,128]{3,2,1,0:T(8,128)S(1)}, f32[2,32,128,128]{3,2,1,0:T(8,128)}, u32[]{:S(2)}) copy-start(f32[2,32,128,128]{3,2,1,0:T(8,128)} %get-tuple-element.65) | copy-start | bytes 12582916
  (7 other events, 34.9 us)
where the time goes:
time: 1060 us; the launch traced here: 1040 us
  waiting for transfers between devices  507 us (48%)
  matrix products  219 us (21%)
  starting transfers between devices  124 us (12%)
  local copies, waits for them, and re-layouts  74.9 us (7%)
  other arithmetic  67.2 us (6%)
  loops' own time  31.3 us (3%)
  blocking collectives  19.8 us (2%)
    ppermute x11, waiting for transfers between devices, passed_along(): return lax.ppermute(value, axis, pairs)  450 us
    ppermute x11, starting transfers between devices, passed_along(): return lax.ppermute(value, axis, pairs)  89.7 us
    dot_general x5, matrix products, pair_solve(): jnp.dot(field.reshape(pairs * planes * points, count), sine_third.T, prec...  82.4 us
    dot_general x5, matrix products, pair_solve(): jnp.dot(density, sine_third, precision=highest)  49.6 us
    all_to_all x4, waiting for transfers between devices, pair_solve(): lax.all_to_all(coeffs, 'slab', split_axis=2, concat_axis=1, tiled=True)  44.3 us
    dot_general x5, matrix products, pair_solve(): coeffs = jnp.einsum('nxyk,yj->nxjk', coeffs, sine_second, precision=highest)  42 us
    another operation x1, loops' own time, on_device(): lax.fori_loop(2, half, carry_step, (totals, visitors, visit_weight, carri...  31.3 us
    dot_general x5, matrix products, pair_solve(): jnp.einsum('nxjk,yj->nxyk', returned, sine_second, precision=highest)  30 us
  transfers between devices with their start and end apart: 20, of which 11 were waited for; matrix products, arithmetic and copies ran while one was open for 25% of the time, Pallas kernels for 0%

commit v1 on v0

--- a/solution.py
+++ b/solution.py
@@ -1,7 +1,16 @@
+import functools
+import math
+
 import jax
 import jax.numpy as jnp
+import numpy as np
 from jax import lax
+from jax.experimental import pallas as pl
+from jax.experimental.pallas import tpu as pltpu
 from jax.sharding import PartitionSpec as P
+
+LANES = 128
+ROWS = 8
 
 
 def passed_along(value, axis, steps):
@@ -26,7 +35,7 @@
     return 1.0 / (1.0 + squares.astype(jnp.float32) / jnp.float32(points * points))
 
 
-def on_device(orbitals, slot_ids, occupations, mode_lists):
+def visiting_form(orbitals, slot_ids, occupations, mode_lists):
     highest = lax.Precision.HIGHEST
     planes = orbitals.shape[1]
     points = orbitals.shape[2]
@@ -107,6 +116,225 @@
     return totals
 
 
+def split_two(value):
+    high = value.astype(jnp.bfloat16)
+    return high, (value - high.astype(jnp.float32)).astype(jnp.bfloat16)
+
+
+def split_table(value):
+    high = lax.reduce_precision(value, exponent_bits=8, mantissa_bits=7)
+    return high.astype(jnp.bfloat16), (value - high).astype(jnp.bfloat16)
+
+
+def mxu(left, right):
+    return jnp.dot(left, right, preferred_element_type=jnp.float32)
+
+
+def windows(count):
+    pack = LANES // math.gcd(count, LANES)
+    tiles = pack * count // LANES
+    return [min(2 * k * count // LANES, tiles - 2) for k in range(pack // 2)], pack, tiles
+
+
+def forward_kernel(firsts, seconds, orbs, left, place_high, place_low, out):
+    planes = orbs.shape[1]
+    count = left.shape[0] // 2
+    starts, pack, lane_tiles = windows(count)
+    row_tiles = count // ROWS
+    per_group = lane_tiles * row_tiles
+    share = out.shape[2]
+    groups = firsts.shape[0] // pack
+
+    for tile in range(groups * per_group, out.shape[0] * share):
+        out[tile // share, :, tile % share] = jnp.zeros((planes,) + out.shape[3:], jnp.float32)
+
+    def group_step(group, _):
+        sums = [None] * lane_tiles
+        for couple, start in enumerate(starts):
+            rows = []
+            for plane in range(planes):
+                sides = []
+                for member in range(2):
+                    slot = group * pack + 2 * couple + member
+                    sides.append(orbs[firsts[slot], plane] * orbs[seconds[slot], plane])
+                high, low = split_two(jnp.concatenate(sides, axis=1))
+                half = mxu(left[...], jnp.concatenate([high, low], axis=0))
+                rows.append(half[:count] + half[count:])
+            high, low = split_two(jnp.concatenate(rows, axis=0))
+            done = (
+                mxu(high, place_high[couple])
+                + mxu(low, place_high[couple])
+                + mxu(high, place_low[couple])
+            )
+            for side in range(2):
+                part = done[:, side * LANES : (side + 1) * LANES]
+                held = sums[start + side]
+                sums[start + side] = part if held is None else held + part
+        for lane_tile in range(lane_tiles):
+            for row_tile in range(row_tiles):
+                tile = group * per_group + lane_tile * row_tiles + row_tile
+                for plane in range(planes):
+                    row = plane * count + row_tile * ROWS
+                    out[tile // share, plane, tile % share] = sums[lane_tile][row : row + ROWS]
+        return 0
+
+    lax.fori_loop(0, groups, group_step, 0)
+
+
+def inverse_kernel(firsts, seconds, weights, field, orbs, left, place_high, place_low, out):
+    planes = orbs.shape[1]
+    count = left.shape[1] // 3
+    starts, pack, lane_tiles = windows(count)
+    row_tiles = count // ROWS
+    per_group = lane_tiles * row_tiles
+    share = field.shape[2]
+    groups = firsts.shape[0] // pack
+    points = orbs.shape[3]
+
+    out[...] = jnp.zeros(out.shape, out.dtype)
+
+    def group_step(group, _):
+        parts = []
+        for lane_tile in range(lane_tiles):
+            rows = []
+            for plane in range(planes):
+                for row_tile in range(row_tiles):
+                    tile = group * per_group + lane_tile * row_tiles + row_tile
+                    rows.append(field[tile // share, plane, tile % share])
+            parts.append(split_two(jnp.concatenate(rows, axis=0)))
+        for couple, start in enumerate(starts):
+            high = jnp.concatenate([parts[start][0], parts[start + 1][0]], axis=1)
+            low = jnp.concatenate([parts[start][1], parts[start + 1][1]], axis=1)
+            half_high, half_low = split_two(
+                mxu(high, place_high[couple])
+                + mxu(low, place_high[couple])
+                + mxu(high, place_low[couple])
+            )
+            for plane in range(planes):
+                span = slice(plane * count, (plane + 1) * count)
+                stacked = jnp.concatenate(
+                    [half_high[span], half_low[span], half_high[span]], axis=0
+                )
+                solved = mxu(left[...], stacked)
+                for member in range(2):
+                    slot = group * pack + 2 * couple + member
+                    one, two = firsts[slot], seconds[slot]
+                    potential = solved[:, member * points : (member + 1) * points]
+                    twice = jnp.where(one == two, 0.0, weights[one])
+                    out[one, plane] += potential * orbs[two, plane] * weights[two]
+                    out[two, plane] += potential * orbs[one, plane] * twice
+        return 0
+
+    lax.fori_loop(0, groups, group_step, 0)
+
+
+def spread_form(orbitals, slot_ids, occupations, mode_lists):
+    bands, slabs = lax.axis_size("band"), lax.axis_size("slab")
+    devices = bands * slabs
+    points = orbitals.shape[2]
+    total = orbitals.shape[0] * bands
+    planes = orbitals.shape[1] // bands
+    count = mode_lists.shape[1]
+    sine_first = sine_table(mode_lists[0], points)
+    sine_second = sine_table(mode_lists[1], points)
+    sine_third = sine_table(mode_lists[2], points)
+    starts, pack, lane_tiles = windows(count)
+    row_tiles = count // ROWS
+    per_group = lane_tiles * row_tiles
+
+    pairs = [(i, j) for i in range(total) for j in range(i, total)]
+    groups = len(pairs) // pack
+    share = -(-groups * per_group // devices)
+    firsts = jnp.asarray(np.array([p[0] for p in pairs], np.int32))
+    seconds = jnp.asarray(np.array([p[1] for p in pairs], np.int32))
+
+    catalog = jnp.arange(occupations.shape[0], dtype=jnp.int32)
+    own_weight = jnp.sum(
+        jnp.where(slot_ids[:, None] == catalog[None, :], occupations[None, :], 0.0), axis=1
+    )
+    weights = lax.all_gather(own_weight, "band", tiled=True)
+
+    spread = lax.all_to_all(orbitals, "band", split_axis=1, concat_axis=0, tiled=True)
+
+    second_high, second_low = split_table(sine_second)
+    empty = jnp.zeros_like(second_low)
+    forward_left = jnp.concatenate(
+        [
+            jnp.concatenate([second_high, second_high], axis=0),
+            jnp.concatenate([second_low, empty], axis=0),
+        ],
+        axis=1,
+    ).T
+    inverse_left = jnp.concatenate([second_high, second_high, second_low], axis=1)
+    placed = []
+    block = jnp.kron(jnp.eye(2, dtype=jnp.float32), sine_third.T)
+    for couple, start in enumerate(starts):
+        above = 2 * couple * count - start * LANES
+        placed.append(jnp.pad(block, ((above, 2 * LANES - above - 2 * count), (0, 0))))
+    inverse_place = split_table(jnp.stack(placed))
+    forward_place = [part.swapaxes(1, 2) for part in inverse_place]
+
+    vmem = pl.BlockSpec(memory_space=pltpu.VMEM)
+    smem = pl.BlockSpec(memory_space=pltpu.SMEM)
+    params = pltpu.CompilerParams(vmem_limit_bytes=50 * 2**20)
+    modal_shape = (devices, planes, share, ROWS, LANES)
+    coeffs = pl.pallas_call(
+        forward_kernel,
+        out_shape=jax.ShapeDtypeStruct(modal_shape, jnp.float32),
+        in_specs=[smem, smem] + [vmem] * 4,
+        out_specs=vmem,
+        compiler_params=params,
+    )(firsts, seconds, spread, forward_left, *forward_place)
+
+    both = ("band", "slab")
+    coeffs = lax.all_to_all(coeffs, both, split_axis=0, concat_axis=0, tiled=True)
+
+    first_sent = (
+        sine_first.reshape(slabs, bands, planes, count).swapaxes(0, 1).reshape(points, count)
+    )
+    squares = [(mode_lists[d] + 1) ** 2 for d in range(3)]
+    inner = (
+        squares[1].reshape(1, row_tiles, ROWS, 1)
+        + jnp.tile(squares[2], pack).reshape(lane_tiles, 1, 1, LANES)
+    ).reshape(per_group, ROWS, LANES)
+    rounds = -(-share // per_group) + 1
+    device = lax.axis_index("band") * slabs + lax.axis_index("slab")
+    inner = lax.dynamic_slice_in_dim(
+        jnp.tile(inner, (rounds, 1, 1)), lax.rem(device * share, per_group), share
+    )
+    both_squares = (squares[0][:, None] + inner.reshape(1, -1)).astype(jnp.float32)
+    screen = 1.0 / (1.0 + both_squares / jnp.float32(points * points))
+    flat = coeffs.reshape(points, share * ROWS * LANES)
+    spectral = screen * jnp.einsum("xm,xa->am", flat, first_sent, precision=lax.Precision.HIGH)
+    spatial = jnp.einsum("am,xa->xm", spectral, first_sent, precision=lax.Precision.HIGH)
+    spatial = spatial.reshape(modal_shape)
+    field = lax.all_to_all(spatial, both, split_axis=0, concat_axis=0, tiled=True)
+
+    terms = pl.pallas_call(
+        inverse_kernel,
+        out_shape=jax.ShapeDtypeStruct(spread.shape, jnp.float32),
+        in_specs=[smem] * 3 + [vmem] * 5,
+        out_specs=vmem,
+        compiler_params=params,
+    )(firsts, seconds, weights, field, spread, inverse_left, *inverse_place)
+    return lax.all_to_all(terms, "band", split_axis=0, concat_axis=1, tiled=True)
+
+
+def on_device(orbitals, slot_ids, occupations, mode_lists):
+    total = orbitals.shape[0] * lax.axis_size("band")
+    points, count = orbitals.shape[2], mode_lists.shape[1]
+    pack = LANES // math.gcd(count, LANES)
+    fits = (
+        orbitals.shape[1] % lax.axis_size("band") == 0
+        and points == LANES
+        and count % 16 == 0
+        and pack * count >= 2 * LANES
+        and (total * (total + 1) // 2) % pack == 0
+    )
+    form = spread_form if fits else visiting_form
+    return form(orbitals, slot_ids, occupations, mode_lists)
+
+
 def solution(mesh):
     in_specs = (P("band", "slab", None, None), P("band"), P(), P())
     out_specs = P("band", "slab", None, None)

time: 1060 us -> 535 us (0.50); the launches traced: 1040 us -> 534 us
  waiting for transfers between devices: 507 us -> 224 us
  matrix products: 219 us -> 7.14 us
  blocking collectives: 19.8 us -> 202 us
  starting transfers between devices: 124 us -> 16.3 us
  other arithmetic: 67.2 us -> 1.31 us
  Pallas kernels: 0 us -> 57.6 us
  local copies, waits for them, and re-layouts: 74.9 us -> 25.2 us
  loops' own time: 31.3 us -> 0 us
    ppermute x11 -> x0, waiting for transfers between devices: 450 us -> none  [passed_along(): return lax.ppermute(value, axis, pairs)]
    dot_general x30 -> x2, matrix products: 219 us -> 7.14 us  [the longest x1 4.48 us: spread_form(): jnp.einsum('xm,xa->am', flat, first_sent, precision=lax.Precision.HIGH)]
    all_to_all x9 -> x3, waiting for transfers between devices: 56.6 us -> 224 us  [the longest x1 116 us: spread_form(): lax.all_to_all(coeffs, both, split_axis=0, concat_axis=0, tiled=True)]
    unnamed x0 -> x1, blocking collectives: none -> 99.6 us
    ppermute x11 -> x0, starting transfers between devices: 89.7 us -> none  [passed_along(): return lax.ppermute(value, axis, pairs)]
    all_to_all x1, blocking collectives: 19.8 us -> 102 us  [spread_form(): lax.all_to_all(terms, 'band', split_axis=0, concat_axis=1, tiled=True)]
    pallas_call x0 -> x2, Pallas kernels: none -> 57.6 us  [the longest x1 34.4 us: spread_form(): pl.pallas_call(inverse_kernel, out_shape=jax.ShapeDtypeStruct(spread.shap...]
    reshape x20 -> x1, local copies, waits for them, and re-layouts: 47.6 us -> 5.57 us  [spread_form(): flat = coeffs.reshape(points, share * ROWS * LANES)]
  transfers between devices with their start and end apart: 20 -> 3, of which waited for: 11 -> 3; matrix products, arithmetic and copies ran while one was open for 25% -> 1% of each run, Pallas kernels for 0% -> 0%
where the time goes in v1:
time: 535 us; the launch traced here: 534 us
  waiting for transfers between devices  224 us (42%)
  blocking collectives  202 us (38%)
  Pallas kernels  57.6 us (11%)
  local copies, waits for them, and re-layouts  25.2 us (5%)
  starting transfers between devices  16.3 us (3%)
  matrix products  7.14 us (1%)
    all_to_all x1, waiting for transfers between devices, spread_form(): lax.all_to_all(coeffs, both, split_axis=0, concat_axis=0, tiled=True)  116 us
    all_to_all x1, blocking collectives, spread_form(): lax.all_to_all(terms, 'band', split_axis=0, concat_axis=1, tiled=True)  102 us
    unnamed x1, blocking collectives  99.6 us
    all_to_all x1, waiting for transfers between devices, spread_form(): lax.all_to_all(orbitals, 'band', split_axis=1, concat_axis=0, tiled=True)  91.7 us
    pallas_call x1, Pallas kernels, spread_form(): pl.pallas_call(inverse_kernel, out_shape=jax.ShapeDtypeStruct(spread.shap...  34.4 us
    pallas_call x1, Pallas kernels, spread_form(): pl.pallas_call(forward_kernel, out_shape=jax.ShapeDtypeStruct(modal_shape...  23.2 us
    all_to_all x1, waiting for transfers between devices, spread_form(): lax.all_to_all(spatial, both, split_axis=0, concat_axis=0, tiled=True)  15.7 us
  transfers between devices with their start and end apart: 3, of which 3 were waited for; matrix products, arithmetic and copies ran while one was open for 1% of the time, Pallas kernels for 0%

profile of v1, /device:TPU:0, one launch (start us, length us, event | category | flops | bytes accessed | tf_op | source)
XLA Modules:
  0.0 533.9 jit_solution(13542736103320072204)
XLA Ops:
  0.0 4.7 copy.38
  4.7 7.4 %all-to-all-start = ((f32[2,32,128,128]{3,2,0,1:T(8,128)}), f32[2,32,128,128]{3,2,0,1:T(8,128)}, u32[]{:S(2)}, u32[]{:S(2)}) async-start(f32[2,32,128,128]{3,2,0,1:T(8,128)} %copy.38), calls=%async_computation | async-start | bytes 8388608 | tf_op jit(solution)/shard_map/all_to_all | solution.py:257
  12.1 0.2 fusion.50
  12.3 0.1 broadcast_multiply_fusion
  12.5 0.2 fusion.4
  12.7 0.2 copy.41.place_high
  12.9 0.2 copy.42.place_low
  13.1 0.3 reduce-precision_convert_fusion.1
  13.5 0.1 fusion.23
  13.6 0.1 copy.40.left
  13.7 91.7 %all-to-all-done = f32[2,32,128,128]{3,2,0,1:T(8,128)} async-done(((f32[2,32,128,128]{3,2,0,1:T(8,128)}), f32[2,32,128,128]{3,2,0,1:T(8,128)}, u32[]{:S(2)}, u32[]{:S(2)}) %all-to-all-start) | async-done | bytes 4194336 | tf_op jit(solution)/shard_map/all_to_all | solution.py:257
  105.4 4.7 copy.39
  110.1 23.2 %shard_map.64 = f32[32,4,10,8,128]{4,3,2,1,0:T(8,128)} custom-call(s32[136]{0:T(256)S(1)} %copy-done, s32[136]{0:T(256)S(1)} %copy-done.1, f32[16,4,128,128]{3,2,1,0:T(8,128)} %bitcast.60, bf16[96,256]{1,0:T(8,128)(2,1)S(1)} %copy.40.left, bf16[4,256,256]{2,1,0:T(8,128)(2,1)S(1)} %copy.41.place_high, bf16[4,256,256]{2,1,0:T(8,128)(2,1)S(1)} %copy.42.place_low), custom_call_target="tpu_custom_call" | custom-call | tf_op jit(solution)/shard_map/pallas_call | solution.py:281
  133.3 3.8 all-to-all-start.1
  137.3 0.1 copy.37
  137.5 0.1 add.167
  138.0 116.3 %all-to-all-done.1 = f32[32,4,10,8,128]{4,3,2,1,0:T(8,128)} async-done(((f32[32,4,10,8,128]{4,3,2,1,0:T(8,128)}), f32[32,4,10,8,128]{4,3,2,1,0:T(8,128)}, u32[]{:S(2)}, u32[]{:S(2)}) %all-to-all-start.1) | async-done | bytes 5242912 | tf_op jit(solution)/shard_map/all_to_all | solution.py:290
  254.3 5.6 %reshape.125 = f32[128,10240]{1,0:T(8,128)} reshape(f32[32,4,10,8,128]{4,3,2,1,0:T(8,128)} %all-to-all-done.1) | data formatting | bytes 10485760 | tf_op jit(solution)/shard_map/reshape | solution.py:307
  259.8 4.5 fusion.3
  264.3 0.3 copy.48
  264.7 2.7 fusion
  267.4 5.4 %copy.44 = f32[32,4,10,8,128]{4,3,2,1,0:T(8,128)} copy(f32[32,4,10,8,128]{4,0,3,2,1:T(8,128)S(1)} %fusion) | data formatting | bytes 10485760 | tf_op jit(solution)/shard_map/am,xa->xm/dot_general | solution.py:309
  272.7 5.1 all-to-all-start.2
  277.9 0.7 dynamic-slice
  279.2 0.2 fusion.54
  279.4 0.2 dynamic-update-slice
  279.7 99.6 %all-reduce.5.weights = f32[16]{0:T(128)S(1)} all-reduce(f32[16]{0:T(128)S(1)} %dynamic-update-slice), channel_id=1, replica_groups=mesh['band'=8,'slab'=4] {'band'}, use_global_device_ids=true, to_apply=%add.5 | all-reduce | flops 16 | bytes 128
  379.3 0.1 pad_maximum_fusion.1.left
  379.4 15.7 %all-to-all-done.2.field = f32[32,4,10,8,128]{4,3,2,1,0:T(8,128)} async-done(((f32[32,4,10,8,128]{4,3,2,1,0:T(8,128)}), f32[32,4,10,8,128]{4,3,2,1,0:T(8,128)}, u32[]{:S(2)}, u32[]{:S(2)}) %all-to-all-start.2) | async-done | bytes 5242912 | tf_op jit(solution)/shard_map/all_to_all | solution.py:311
  395.1 34.4 %shard_map.65 = f32[16,4,128,128]{3,2,1,0:T(8,128)} custom-call(s32[136]{0:T(256)S(1)} %copy-done, s32[136]{0:T(256)S(1)} %copy-done.1, f32[16]{0:T(128)S(1)} %all-reduce.5.weights, f32[32,4,10,8,128]{4,3,2,1,0:T(8,128)} %all-to-all-done.2.field, f32[16,4,128,128]{3,2,1,0:T(8,128)} %bitcast.61, bf16[128,144]{1,0:T(8,128)(2,1)S(1)} %pad_maximum_fusion.1.left, ...), custom_call_target="tpu_custom_call" | custom-call | tf_op jit(solution)/shard_map/pallas_call | solution.py:313
  429.5 102.1 %all_to_all.46 = f32[16,4,128,128]{3,2,1,0:T(8,128)S(1)} all-to-all(f32[16,4,128,128]{3,2,1,0:T(8,128)} %shard_map.65), channel_id=1, replica_groups=mesh['band'=8,'slab'=4] {'band'}, dimensions={0} | all-to-all | bytes 8388608 | tf_op jit(solution)/shard_map/all_to_all | solution.py:320
  531.6 2.3 copy.45
  (35 shorter events, 0.8 us)
Async XLA Ops:
  4.7 7.4 %copy-start.2 = (s32[3,48]{1,0:T(4,128)S(1)}, s32[3,48]{1,0:T(4,128)}, u32[]{:S(2)}) copy-start(s32[3,48]{1,0:T(4,128)} %param.9) | copy-start | bytes 1732
  4.7 100.7 %all-to-all-start = ((f32[2,32,128,128]{3,2,0,1:T(8,128)}), f32[2,32,128,128]{3,2,0,1:T(8,128)}, u32[]{:S(2)}, u32[]{:S(2)}) async-start(f32[2,32,128,128]{3,2,0,1:T(8,128)} %copy.38), calls=%async_computation | async-start | bytes 8388608 | tf_op jit(solution)/shard_map/all_to_all | solution.py:257
  105.4 4.7 copy-start
  105.4 4.7 copy-start.1
  133.3 121.0 %all-to-all-start.1 = ((f32[32,4,10,8,128]{4,3,2,1,0:T(8,128)}), f32[32,4,10,8,128]{4,3,2,1,0:T(8,128)}, u32[]{:S(2)}, u32[]{:S(2)}) async-start(f32[32,4,10,8,128]{4,3,2,1,0:T(8,128)} %shard_map.64), calls=%async_computation.1 | async-start | bytes 10485760 | tf_op jit(solution)/shard_map/all_to_all | solution.py:290
  272.7 5.1 copy-start.5
  272.7 6.5 %copy-start.3 = (f32[16]{0:T(128)S(1)}, f32[16]{0:T(128)}, u32[]{:S(2)}) copy-start(f32[16]{0:T(128)} %param.8) | copy-start | bytes 196
  272.7 6.5 %copy-start.4 = (s32[2]{0:T(128)S(1)}, s32[2]{0:T(128)}, u32[]{:S(2)}) copy-start(s32[2]{0:T(128)} %param.7) | copy-start | bytes 28
  272.7 122.4 %all-to-all-start.2 = ((f32[32,4,10,8,128]{4,3,2,1,0:T(8,128)}), f32[32,4,10,8,128]{4,3,2,1,0:T(8,128)}, u32[]{:S(2)}, u32[]{:S(2)}) async-start(f32[32,4,10,8,128]{4,3,2,1,0:T(8,128)} %copy.44), calls=%async_computation.2 | async-start | bytes 10485760 | tf_op jit(solution)/shard_map/all_to_all | solution.py:311

commit v2 on v1

--- a/solution.py
+++ b/solution.py
@@ -136,7 +136,7 @@
     return [min(2 * k * count // LANES, tiles - 2) for k in range(pack // 2)], pack, tiles
 
 
-def forward_kernel(firsts, seconds, orbs, left, place_high, place_low, out):
+def forward_kernel(firsts, seconds, orbs, others, left, place_high, place_low, out):
     planes = orbs.shape[1]
     count = left.shape[0] // 2
     starts, pack, lane_tiles = windows(count)
@@ -156,7 +156,7 @@
                 sides = []
                 for member in range(2):
                     slot = group * pack + 2 * couple + member
-                    sides.append(orbs[firsts[slot], plane] * orbs[seconds[slot], plane])
+                    sides.append(orbs[firsts[slot], plane] * others[seconds[slot], plane])
                 high, low = split_two(jnp.concatenate(sides, axis=1))
                 half = mxu(left[...], jnp.concatenate([high, low], axis=0))
                 rows.append(half[:count] + half[count:])
@@ -181,7 +181,8 @@
     lax.fori_loop(0, groups, group_step, 0)
 
 
-def inverse_kernel(firsts, seconds, weights, field, orbs, left, place_high, place_low, out):
+def inverse_kernel(mutual, firsts, seconds, scale_one, scale_two, field, orbs, others, *rest):
+    *base, left, place_high, place_low, out = rest
     planes = orbs.shape[1]
     count = left.shape[1] // 3
     starts, pack, lane_tiles = windows(count)
@@ -191,7 +192,7 @@
     groups = firsts.shape[0] // pack
     points = orbs.shape[3]
 
-    out[...] = jnp.zeros(out.shape, out.dtype)
+    out[...] = base[0][...] if base else jnp.zeros(out.shape, out.dtype)
 
     def group_step(group, _):
         parts = []
@@ -220,9 +221,9 @@
                     slot = group * pack + 2 * couple + member
                     one, two = firsts[slot], seconds[slot]
                     potential = solved[:, member * points : (member + 1) * points]
-                    twice = jnp.where(one == two, 0.0, weights[one])
-                    out[one, plane] += potential * orbs[two, plane] * weights[two]
-                    out[two, plane] += potential * orbs[one, plane] * twice
+                    out[one, plane] += potential * others[two, plane] * scale_one[slot]
+                    if mutual:
+                        out[two, plane] += potential * orbs[one, plane] * scale_two[slot]
         return 0
 
     lax.fori_loop(0, groups, group_step, 0)
@@ -230,10 +231,12 @@
 
 def spread_form(orbitals, slot_ids, occupations, mode_lists):
     bands, slabs = lax.axis_size("band"), lax.axis_size("slab")
-    devices = bands * slabs
+    half = bands // 2
+    devices = half * slabs
     points = orbitals.shape[2]
-    total = orbitals.shape[0] * bands
-    planes = orbitals.shape[1] // bands
+    local = orbitals.shape[0]
+    own = local * half
+    planes = orbitals.shape[1] // half
     count = mode_lists.shape[1]
     sine_first = sine_table(mode_lists[0], points)
     sine_second = sine_table(mode_lists[1], points)
@@ -241,20 +244,35 @@
     starts, pack, lane_tiles = windows(count)
     row_tiles = count // ROWS
     per_group = lane_tiles * row_tiles
-
-    pairs = [(i, j) for i in range(total) for j in range(i, total)]
-    groups = len(pairs) // pack
-    share = -(-groups * per_group // devices)
-    firsts = jnp.asarray(np.array([p[0] for p in pairs], np.int32))
-    seconds = jnp.asarray(np.array([p[1] for p in pairs], np.int32))
+    band, slab = lax.axis_index("band"), lax.axis_index("slab")
+    sides = [[side * half + member for member in range(half)] for side in range(2)]
+    all_sides = [
+        [member * slabs + other for member in side for other in range(slabs)] for side in sides
+    ]
+    both = ("band", "slab")
+
+    def to_planes(value):
+        return lax.all_to_all(
+            value, "band", split_axis=1, concat_axis=0, tiled=True, axis_index_groups=sides
+        )
+
+    def exchanged(value):
+        return lax.all_to_all(
+            value, both, split_axis=0, concat_axis=0, tiled=True, axis_index_groups=all_sides
+        )
+
+    visiting = [passed_along(orbitals[k : k + 1], "band", half) for k in range(local)]
+    mine = to_planes(orbitals)
+    visiting = [to_planes(value) for value in visiting]
 
     catalog = jnp.arange(occupations.shape[0], dtype=jnp.int32)
     own_weight = jnp.sum(
         jnp.where(slot_ids[:, None] == catalog[None, :], occupations[None, :], 0.0), axis=1
     )
-    weights = lax.all_gather(own_weight, "band", tiled=True)
-
-    spread = lax.all_to_all(orbitals, "band", split_axis=1, concat_axis=0, tiled=True)
+    weights = lax.all_gather(own_weight, "band", tiled=True).reshape(2, own)
+    upper = band >= half
+    my_weights = jnp.where(upper, weights[1], weights[0])
+    other_weights = jnp.where(upper, weights[0], weights[1]).reshape(half, local)
 
     second_high, second_low = split_table(sine_second)
     empty = jnp.zeros_like(second_low)
@@ -274,62 +292,97 @@
     inverse_place = split_table(jnp.stack(placed))
     forward_place = [part.swapaxes(1, 2) for part in inverse_place]
 
+    first_sent = (
+        sine_first.reshape(slabs, half, planes, count).swapaxes(0, 1).reshape(points, count)
+    )
+    squares = [(mode_lists[d] + 1) ** 2 for d in range(3)]
+    inner_tiles = (
+        squares[1].reshape(1, row_tiles, ROWS, 1)
+        + jnp.tile(squares[2], pack).reshape(lane_tiles, 1, 1, LANES)
+    ).reshape(per_group, ROWS, LANES)
+    device = lax.rem(band, half) * slabs + slab
+
     vmem = pl.BlockSpec(memory_space=pltpu.VMEM)
     smem = pl.BlockSpec(memory_space=pltpu.SMEM)
     params = pltpu.CompilerParams(vmem_limit_bytes=50 * 2**20)
-    modal_shape = (devices, planes, share, ROWS, LANES)
-    coeffs = pl.pallas_call(
-        forward_kernel,
-        out_shape=jax.ShapeDtypeStruct(modal_shape, jnp.float32),
-        in_specs=[smem, smem] + [vmem] * 4,
-        out_specs=vmem,
-        compiler_params=params,
-    )(firsts, seconds, spread, forward_left, *forward_place)
-
-    both = ("band", "slab")
-    coeffs = lax.all_to_all(coeffs, both, split_axis=0, concat_axis=0, tiled=True)
-
-    first_sent = (
-        sine_first.reshape(slabs, bands, planes, count).swapaxes(0, 1).reshape(points, count)
-    )
-    squares = [(mode_lists[d] + 1) ** 2 for d in range(3)]
-    inner = (
-        squares[1].reshape(1, row_tiles, ROWS, 1)
-        + jnp.tile(squares[2], pack).reshape(lane_tiles, 1, 1, LANES)
-    ).reshape(per_group, ROWS, LANES)
-    rounds = -(-share // per_group) + 1
-    device = lax.axis_index("band") * slabs + lax.axis_index("slab")
-    inner = lax.dynamic_slice_in_dim(
-        jnp.tile(inner, (rounds, 1, 1)), lax.rem(device * share, per_group), share
-    )
-    both_squares = (squares[0][:, None] + inner.reshape(1, -1)).astype(jnp.float32)
-    screen = 1.0 / (1.0 + both_squares / jnp.float32(points * points))
-    flat = coeffs.reshape(points, share * ROWS * LANES)
-    spectral = screen * jnp.einsum("xm,xa->am", flat, first_sent, precision=lax.Precision.HIGH)
-    spatial = jnp.einsum("am,xa->xm", spectral, first_sent, precision=lax.Precision.HIGH)
-    spatial = spatial.reshape(modal_shape)
-    field = lax.all_to_all(spatial, both, split_axis=0, concat_axis=0, tiled=True)
-
-    terms = pl.pallas_call(
-        inverse_kernel,
-        out_shape=jax.ShapeDtypeStruct(spread.shape, jnp.float32),
-        in_specs=[smem] * 3 + [vmem] * 5,
-        out_specs=vmem,
-        compiler_params=params,
-    )(firsts, seconds, weights, field, spread, inverse_left, *inverse_place)
-    return lax.all_to_all(terms, "band", split_axis=0, concat_axis=1, tiled=True)
+
+    def modal(coeffs):
+        share = coeffs.shape[2]
+        rounds = -(-share // per_group) + 1
+        inner = lax.dynamic_slice_in_dim(
+            jnp.tile(inner_tiles, (rounds, 1, 1)), lax.rem(device * share, per_group), share
+        )
+        both_squares = (squares[0][:, None] + inner.reshape(1, -1)).astype(jnp.float32)
+        screen = 1.0 / (1.0 + both_squares / jnp.float32(points * points))
+        flat = exchanged(coeffs).reshape(points, share * ROWS * LANES)
+        spectral = screen * jnp.einsum(
+            "xm,xa->am", flat, first_sent, precision=lax.Precision.HIGH
+        )
+        spatial = jnp.einsum("am,xa->xm", spectral, first_sent, precision=lax.Precision.HIGH)
+        return exchanged(spatial.reshape(coeffs.shape))
+
+    def pair_cost(pairs):
+        work = pairs * planes * points * points * 2 * LANES * 4
+        return pl.CostEstimate(flops=work, bytes_accessed=2**24, transcendentals=0)
+
+    def fields_of(pairs, others):
+        tables = [jnp.asarray(np.array(part, np.int32)) for part in zip(*pairs)]
+        groups = len(pairs) // pack
+        share = -(-groups * per_group // devices)
+        coeffs = pl.pallas_call(
+            forward_kernel,
+            out_shape=jax.ShapeDtypeStruct((devices, planes, share, ROWS, LANES), jnp.float32),
+            in_specs=[smem] * 2 + [vmem] * 5,
+            out_specs=vmem,
+            compiler_params=params,
+            cost_estimate=pair_cost(len(pairs)),
+        )(*tables, mine, others, forward_left, *forward_place)
+        return tables, modal(coeffs)
+
+    def terms_of(tables, field, others, scales, base):
+        extra = [] if base is None else [base]
+        return pl.pallas_call(
+            functools.partial(inverse_kernel, base is None),
+            out_shape=jax.ShapeDtypeStruct(mine.shape, jnp.float32),
+            in_specs=[smem] * 4 + [vmem] * (6 + len(extra)),
+            out_specs=vmem,
+            compiler_params=params,
+            cost_estimate=pair_cost(tables[0].shape[0]),
+        )(*tables, *scales, field, mine, others, *extra, inverse_left, *inverse_place)
+
+    pairs = [(i, j) for i in range(own) for j in range(i, own)]
+    true_pairs = len(pairs)
+    pairs += [(0, 0)] * (-true_pairs % pack)
+    valid = np.arange(len(pairs)) < true_pairs
+    apart = np.array([i != j for i, j in pairs])
+    tables, field = fields_of(pairs, mine)
+    scales = (
+        jnp.where(valid, my_weights[tables[1]], 0.0),
+        jnp.where(valid & apart, my_weights[tables[0]], 0.0),
+    )
+    cross = [(i, j) for i in range(own) for j in range(half)]
+    solved = [fields_of(cross, value) for value in visiting]
+    terms = terms_of(tables, field, mine, scales, None)
+    for k, (tables, field) in enumerate(solved):
+        scale = other_weights[:, k][tables[1]]
+        terms = terms_of(tables, field, visiting[k], (scale, scale), terms)
+    return lax.all_to_all(
+        terms, "band", split_axis=0, concat_axis=1, tiled=True, axis_index_groups=sides
+    )
 
 
 def on_device(orbitals, slot_ids, occupations, mode_lists):
-    total = orbitals.shape[0] * lax.axis_size("band")
+    bands = lax.axis_size("band")
     points, count = orbitals.shape[2], mode_lists.shape[1]
     pack = LANES // math.gcd(count, LANES)
+    half = bands // 2
     fits = (
-        orbitals.shape[1] % lax.axis_size("band") == 0
+        bands % 2 == 0
+        and orbitals.shape[1] % half == 0
         and points == LANES
         and count % 16 == 0
         and pack * count >= 2 * LANES
-        and (total * (total + 1) // 2) % pack == 0
+        and (orbitals.shape[0] * half * half) % pack == 0
     )
     form = spread_form if fits else visiting_form
     return form(orbitals, slot_ids, occupations, mode_lists)

time: 535 us -> 654 us (1.22)
  waiting for transfers between devices: 224 us -> 341 us
  blocking collectives: 202 us -> 97 us
  starting transfers between devices: 16.3 us -> 51 us
  Pallas kernels: 57.6 us -> 88.6 us
  local copies, waits for them, and re-layouts: 25.2 us -> 43.2 us
  other arithmetic: 1.31 us -> 16.5 us
  matrix products: 7.14 us -> 13.7 us
    ppermute x0 -> x2, waiting for transfers between devices: none -> 177 us  [passed_along(): return lax.ppermute(value, axis, pairs)]
    all_to_all x3 -> x9, waiting for transfers between devices: 224 us -> 164 us  [the longest x6 135 us: exchanged(): lax.all_to_all(value, both, split_axis=0, concat_axis=0, tiled=True, axis...]
    all_to_all x1, blocking collectives: 102 us -> 49.1 us  [spread_form(): lax.all_to_all(terms, 'band', split_axis=0, concat_axis=1, tiled=True, ax...]
    unnamed x1, blocking collectives: 99.6 us -> 47.9 us
    pallas_call x2 -> x6, Pallas kernels: 57.6 us -> 88.6 us  [the longest x3 52.1 us: terms_of(): pl.pallas_call(functools.partial(inverse_kernel, base is None), out_shape...]
    all_to_all x3 -> x9, starting transfers between devices: 16.3 us -> 43.7 us  [the longest x6 30.5 us: exchanged(): lax.all_to_all(value, both, split_axis=0, concat_axis=0, tiled=True, axis...]
    select_n x0 -> x3, other arithmetic: none -> 10.3 us  [the longest x1 5.1 us: spread_form(): jnp.where(valid & apart, my_weights[tables[0]], 0.0)]
    ppermute x0 -> x2, starting transfers between devices: none -> 7.28 us  [passed_along(): return lax.ppermute(value, axis, pairs)]
  transfers between devices with their start and end apart: 3 -> 11, of which waited for: 3 -> 10; matrix products, arithmetic and copies ran while one was open for 1% -> 10% of each run, Pallas kernels for 0% -> 11%
where the time goes in v2:
time: 654 us; the launch traced here: 652 us
  waiting for transfers between devices  341 us (52%)
  blocking collectives  97 us (15%)
  Pallas kernels  88.6 us (14%)
  starting transfers between devices  51 us (8%)
  local copies, waits for them, and re-layouts  43.2 us (7%)
  other arithmetic  16.5 us (3%)
  matrix products  13.7 us (2%)
    ppermute x2, waiting for transfers between devices, passed_along(): return lax.ppermute(value, axis, pairs)  177 us
    all_to_all x6, waiting for transfers between devices, exchanged(): lax.all_to_all(value, both, split_axis=0, concat_axis=0, tiled=True, axis...  135 us
    pallas_call x3, Pallas kernels, terms_of(): pl.pallas_call(functools.partial(inverse_kernel, base is None), out_shape...  52.1 us
    all_to_all x1, blocking collectives, spread_form(): lax.all_to_all(terms, 'band', split_axis=0, concat_axis=1, tiled=True, ax...  49.1 us
    unnamed x1, blocking collectives  47.9 us
    pallas_call x3, Pallas kernels, fields_of(): pl.pallas_call(forward_kernel, out_shape=jax.ShapeDtypeStruct((devices, p...  36.5 us
    all_to_all x6, starting transfers between devices, exchanged(): lax.all_to_all(value, both, split_axis=0, concat_axis=0, tiled=True, axis...  30.5 us
    all_to_all x3, waiting for transfers between devices, to_planes(): lax.all_to_all(value, 'band', split_axis=1, concat_axis=0, tiled=True, ax...  29.2 us
  transfers between devices with their start and end apart: 11, of which 10 were waited for; matrix products, arithmetic and copies ran while one was open for 10% of the time, Pallas kernels for 11%

profile of v2, /device:TPU:0, one launch (start us, length us, event | category | flops | bytes accessed | tf_op | source)
XLA Modules:
  0.0 652.3 jit_solution(9846927012146715436)
XLA Ops:
  4.0 4.0 collective-permute-start
  8.0 90.7 %collective-permute-done = f32[1,32,128,128]{3,2,0,1:T(8,128)} collective-permute-done((f32[1,32,128,128]{3,2,0,1:T(8,128)S(1)}, f32[1,32,128,128]{3,2,0,1:T(8,128)}, u32[]{:S(2)}, u32[]{:S(2)}) %collective-permute-start) | collective-permute-done | bytes 2097184 | tf_op jit(solution)/shard_map/ppermute | solution.py:19
  102.3 4.7 copy.76
  107.0 19.9 %all-to-all-done.1 = f32[1,32,128,128]{3,2,0,1:T(8,128)S(1)} async-done(((f32[1,32,128,128]{3,2,0,1:T(8,128)}), f32[1,32,128,128]{3,2,0,1:T(8,128)S(1)}, u32[]{:S(2)}, u32[]{:S(2)}) %all-to-all-start.1) | async-done | bytes 2097184 | tf_op jit(solution)/shard_map/all_to_all | solution.py:255
  126.9 4.9 all-to-all-start
  135.0 86.4 %collective-permute-done.1 = f32[1,32,128,128]{3,2,0,1:T(8,128)} collective-permute-done((f32[1,32,128,128]{3,2,0,1:T(8,128)}, f32[1,32,128,128]{3,2,0,1:T(8,128)}, u32[]{:S(2)}, u32[]{:S(2)}) %collective-permute-start.1) | collective-permute-done | bytes 2097184 | tf_op jit(solution)/shard_map/ppermute | solution.py:19
  224.2 4.8 all-to-all-start.4
  232.1 4.8 copy.77
  236.9 10.9 %shard_map.118 = f32[16,8,5,8,128]{4,3,2,1,0:T(8,128)} custom-call(s32[32]{0:T(128)S(1)} %copy-done.7, s32[32]{0:T(128)S(1)} %copy-done.6, f32[8,8,128,128]{3,2,1,0:T(8,128)} %bitcast.108, f32[4,8,128,128]{3,2,1,0:T(8,128)S(1)} %bitcast.104, bf16[96,256]{1,0:T(8,128)(2,1)S(1)} %copy.79.left, bf16[4,256,256]{2,1,0:T(8,128)(2,1)S(1)} %copy-done, ...), custom_call_target="tpu_custom_call" | custom-call | flops 4294967296 | bytes 16777216 | tf_op jit(solution)/shard_map/pallas_call | solution.py:332
  247.8 6.5 %all-to-all-done.4 = f32[1,32,128,128]{3,2,0,1:T(8,128)} async-done(((f32[1,32,128,128]{3,2,0,1:T(8,128)}), f32[1,32,128,128]{3,2,0,1:T(8,128)}, u32[]{:S(2)}, u32[]{:S(2)}) %all-to-all-start.4) | async-done | bytes 2097184 | tf_op jit(solution)/shard_map/all_to_all | solution.py:255
  254.3 4.5 all-to-all-start.2
  260.9 11.5 %shard_map.119 = f32[16,8,5,8,128]{4,3,2,1,0:T(8,128)} custom-call(s32[32]{0:T(128)S(1)} %copy-done.7, s32[32]{0:T(128)S(1)} %copy-done.6, f32[8,8,128,128]{3,2,1,0:T(8,128)} %bitcast.109, f32[4,8,128,128]{3,2,1,0:T(8,128)} %bitcast.32.others, bf16[96,256]{1,0:T(8,128)(2,1)S(1)} %copy.79.left, bf16[4,256,256]{2,1,0:T(8,128)(2,1)S(1)} %copy-done.1, ...), custom_call_target="tpu_custom_call" | custom-call | flops 4294967296 | bytes 16777216 | tf_op jit(solution)/shard_map/pallas_call | solution.py:332
  272.4 23.1 %all-to-all-done.2 = f32[16,8,5,8,128]{4,3,2,1,0:T(8,128)} async-done(((f32[16,8,5,8,128]{4,3,2,1,0:T(8,128)}), f32[16,8,5,8,128]{4,3,2,1,0:T(8,128)}, u32[]{:S(2)}, u32[]{:S(2)}) %all-to-all-start.2) | async-done | bytes 2621472 | tf_op jit(solution)/shard_map/all_to_all | solution.py:260
  295.5 4.5 all-to-all-start.5
  302.1 14.1 %shard_map.120 = f32[16,8,6,8,128]{4,3,2,1,0:T(8,128)} custom-call(s32[40]{0:T(128)S(1)} %copy-done.9, s32[40]{0:T(128)S(1)} %copy-done.8, f32[8,8,128,128]{3,2,1,0:T(8,128)} %bitcast.110, f32[8,8,128,128]{3,2,1,0:T(8,128)} %bitcast.111, bf16[96,256]{1,0:T(8,128)(2,1)S(1)} %copy.79.left, bf16[4,256,256]{2,1,0:T(8,128)(2,1)S(1)} %copy-done.2, ...), custom_call_target="tpu_custom_call" | custom-call | flops 5368709120 | bytes 16777216 | tf_op jit(solution)/shard_map/pallas_call | solution.py:332
  316.2 20.5 %all-to-all-done.5 = f32[16,8,5,8,128]{4,3,2,1,0:T(8,128)} async-done(((f32[16,8,5,8,128]{4,3,2,1,0:T(8,128)}), f32[16,8,5,8,128]{4,3,2,1,0:T(8,128)}, u32[]{:S(2)}, u32[]{:S(2)}) %all-to-all-start.5) | async-done | bytes 2621472 | tf_op jit(solution)/shard_map/all_to_all | solution.py:260
  336.7 4.7 all-to-all-start.7
  352.3 32.6 %all-to-all-done.7 = f32[16,8,6,8,128]{4,3,2,1,0:T(8,128)} async-done(((f32[16,8,6,8,128]{4,3,2,1,0:T(8,128)}), f32[16,8,6,8,128]{4,3,2,1,0:T(8,128)}, u32[]{:S(2)}, u32[]{:S(2)}) %all-to-all-start.7) | async-done | bytes 3145760 | tf_op jit(solution)/shard_map/all_to_all | solution.py:260
  384.9 5.7 all-to-all-start.6
  390.6 4.2 reshape.174
  402.3 25.1 %all-to-all-done.6.field = f32[16,8,5,8,128]{4,3,2,1,0:T(8,128)} async-done(((f32[16,8,5,8,128]{4,3,2,1,0:T(8,128)}), f32[16,8,5,8,128]{4,3,2,1,0:T(8,128)}, u32[]{:S(2)}, u32[]{:S(2)}) %all-to-all-start.6) | async-done | bytes 2621472 | tf_op jit(solution)/shard_map/all_to_all | solution.py:260
  427.3 4.8 all-to-all-start.8
  442.3 33.3 %all-to-all-done.8.field = f32[16,8,6,8,128]{4,3,2,1,0:T(8,128)} async-done(((f32[16,8,6,8,128]{4,3,2,1,0:T(8,128)}), f32[16,8,6,8,128]{4,3,2,1,0:T(8,128)}, u32[]{:S(2)}, u32[]{:S(2)}) %all-to-all-start.8) | async-done | bytes 3145760 | tf_op jit(solution)/shard_map/all_to_all | solution.py:260
  475.7 6.5 all-to-all-start.3
  484.0 47.9 %all-reduce.5 = f32[16]{0:T(128)S(1)} all-reduce(f32[16]{0:T(128)S(1)} %dynamic-update-slice), channel_id=1, replica_groups=mesh['band'=8,'slab'=4] {'band'}, use_global_device_ids=true, to_apply=%add.5 | all-reduce | flops 16 | bytes 128
  533.5 4.9 select_select_fusion.2
  538.5 5.1 select_select_fusion.scale_two
  543.7 5.1 select_select_fusion.1.scale_one
  548.8 19.5 %shard_map.121.rest_0_ = f32[8,8,128,128]{3,2,1,0:T(8,128)} custom-call(s32[40]{0:T(128)S(1)} %copy-done.9, s32[40]{0:T(128)S(1)} %copy-done.8, f32[40]{0:T(128)S(1)} %select_select_fusion.1.scale_one, f32[40]{0:T(128)S(1)} %select_select_fusion.scale_two, f32[16,8,6,8,128]{4,3,2,1,0:T(8,128)} %all-to-all-done.8.field, f32[8,8,128,128]{3,2,1,0:T(8,128)} %bitcast.112, ...), custom_call_target="tpu_custom_call" | custom-call | flops 5368709120 | bytes 16777216 | tf_op jit(solution)/shard_map/pallas_call | solution.py:344
  568.3 16.6 %shard_map.122.rest_0_ = f32[8,8,128,128]{3,2,1,0:T(8,128)} custom-call(s32[32]{0:T(128)S(1)} %copy-done.7, s32[32]{0:T(128)S(1)} %copy-done.6, f32[32]{0:T(128)S(1)} %get-tuple-element.27.scale_one.scale_two, f32[32]{0:T(128)S(1)} %get-tuple-element.27.scale_one.scale_two, f32[16,8,5,8,128]{4,3,2,1,0:T(8,128)} %all-to-all-done.6.field, ...), custom_call_target="tpu_custom_call" | custom-call | flops 4294967296 | bytes 16777216 | tf_op jit(solution)/shard_map/pallas_call | solution.py:344
  584.9 16.0 %shard_map.123 = f32[8,8,128,128]{3,2,1,0:T(8,128)} custom-call(s32[32]{0:T(128)S(1)} %copy-done.7, s32[32]{0:T(128)S(1)} %copy-done.6, f32[32]{0:T(128)S(1)} %get-tuple-element.28.scale_one.scale_two, f32[32]{0:T(128)S(1)} %get-tuple-element.28.scale_one.scale_two, f32[16,8,5,8,128]{4,3,2,1,0:T(8,128)} %all-to-all-done.3.field, ...), custom_call_target="tpu_custom_call" | custom-call | flops 4294967296 | bytes 16777216 | tf_op jit(solution)/shard_map/pallas_call | solution.py:344
  600.9 49.1 %all_to_all.90 = f32[8,8,128,128]{3,2,1,0:T(8,128)S(1)} all-to-all(f32[8,8,128,128]{3,2,1,0:T(8,128)} %shard_map.123), channel_id=1, replica_groups={{0,4,8,12},{16,20,24,28},{1,5,9,13},{17,21,25,29},{2,6,10,14},{18,22,26..., dimensions={0} | all-to-all | bytes 8388608 | tf_op jit(solution)/shard_map/all_to_all | solution.py:369
  (128 shorter events, 54.2 us)
Async XLA Ops:
  4.0 94.7 %collective-permute-start = (f32[1,32,128,128]{3,2,0,1:T(8,128)S(1)}, f32[1,32,128,128]{3,2,0,1:T(8,128)}, u32[]{:S(2)}, u32[]{:S(2)}) collective-permute-start(f32[1,32,128,128]{3,2,0,1:T(8,128)S(1)} %get-tuple-element.6), channel_id=1, source_target_pairs={{0,16},{4,20},{8,24},{12,28},{16,0},{20,4},{24,8},{28,12},{1,17},{... | collective-permute-start | bytes 6291464 | tf_op jit(solution)/shard_map/ppermute | solution.py:19
  98.7 28.2 %all-to-all-start.1 = ((f32[1,32,128,128]{3,2,0,1:T(8,128)}), f32[1,32,128,128]{3,2,0,1:T(8,128)S(1)}, u32[]{:S(2)}, u32[]{:S(2)}) async-start(f32[1,32,128,128]{3,2,0,1:T(8,128)} %collective-permute-done), calls=%async_computation.1 | async-start | bytes 4194304 | tf_op jit(solution)/shard_map/all_to_all | solution.py:255
  126.9 97.3 %all-to-all-start = ((f32[2,32,128,128]{3,2,0,1:T(8,128)}), f32[2,32,128,128]{3,2,0,1:T(8,128)}, u32[]{:S(2)}, u32[]{:S(2)}) async-start(f32[2,32,128,128]{3,2,0,1:T(8,128)} %copy.76), calls=%async_computation | async-start | bytes 8388608 | tf_op jit(solution)/shard_map/all_to_all | solution.py:255
  131.8 97.2 %copy-start.10 = (s32[3,48]{1,0:T(4,128)S(1)}, s32[3,48]{1,0:T(4,128)}, u32[]{:S(2)}) copy-start(s32[3,48]{1,0:T(4,128)} %param.15) | copy-start | bytes 1732
  131.8 89.6 %collective-permute-start.1 = (f32[1,32,128,128]{3,2,0,1:T(8,128)}, f32[1,32,128,128]{3,2,0,1:T(8,128)}, u32[]{:S(2)}, u32[]{:S(2)}) collective-permute-start(f32[1,32,128,128]{3,2,0,1:T(8,128)} %get-tuple-element.5), channel_id=1, source_target_pairs={{0,16},{4,20},{8,24},{12,28},{16,0},{20,4},{24,8},{28,12},{1,17},{... | collective-permute-start | bytes 6291464 | tf_op jit(solution)/shard_map/ppermute | solution.py:19
  224.2 30.2 %all-to-all-start.4 = ((f32[1,32,128,128]{3,2,0,1:T(8,128)}), f32[1,32,128,128]{3,2,0,1:T(8,128)}, u32[]{:S(2)}, u32[]{:S(2)}) async-start(f32[1,32,128,128]{3,2,0,1:T(8,128)} %collective-permute-done.1), calls=%async_computation.4 | async-start | bytes 4194304 | tf_op jit(solution)/shard_map/all_to_all | solution.py:255
  254.3 41.2 %all-to-all-start.2 = ((f32[16,8,5,8,128]{4,3,2,1,0:T(8,128)}), f32[16,8,5,8,128]{4,3,2,1,0:T(8,128)}, u32[]{:S(2)}, u32[]{:S(2)}) async-start(f32[16,8,5,8,128]{4,3,2,1,0:T(8,128)} %shard_map.118), calls=%async_computation.2 | async-start | bytes 5242880 | tf_op jit(solution)/shard_map/all_to_all | solution.py:260
  295.5 41.2 %all-to-all-start.5 = ((f32[16,8,5,8,128]{4,3,2,1,0:T(8,128)}), f32[16,8,5,8,128]{4,3,2,1,0:T(8,128)}, u32[]{:S(2)}, u32[]{:S(2)}) async-start(f32[16,8,5,8,128]{4,3,2,1,0:T(8,128)} %shard_map.119), calls=%async_computation.5 | async-start | bytes 5242880 | tf_op jit(solution)/shard_map/all_to_all | solution.py:260
  336.7 48.2 %all-to-all-start.7 = ((f32[16,8,6,8,128]{4,3,2,1,0:T(8,128)}), f32[16,8,6,8,128]{4,3,2,1,0:T(8,128)}, u32[]{:S(2)}, u32[]{:S(2)}) async-start(f32[16,8,6,8,128]{4,3,2,1,0:T(8,128)} %shard_map.120), calls=%async_computation.7 | async-start | bytes 6291456 | tf_op jit(solution)/shard_map/all_to_all | solution.py:260
  384.9 42.4 %all-to-all-start.6 = ((f32[16,8,5,8,128]{4,3,2,1,0:T(8,128)}), f32[16,8,5,8,128]{4,3,2,1,0:T(8,128)}, u32[]{:S(2)}, u32[]{:S(2)}) async-start(f32[16,8,5,8,128]{4,3,2,1,0:T(8,128)} %copy.89), calls=%async_computation.6 | async-start | bytes 5242880 | tf_op jit(solution)/shard_map/all_to_all | solution.py:260
  427.3 48.3 %all-to-all-start.8 = ((f32[16,8,6,8,128]{4,3,2,1,0:T(8,128)}), f32[16,8,6,8,128]{4,3,2,1,0:T(8,128)}, u32[]{:S(2)}, u32[]{:S(2)}) async-start(f32[16,8,6,8,128]{4,3,2,1,0:T(8,128)} %copy.94), calls=%async_computation.8 | async-start | bytes 6291456 | tf_op jit(solution)/shard_map/all_to_all | solution.py:260
  442.1 41.4 %copy-start.31 = (s32[2]{0:T(128)S(1)}, s32[2]{0:T(128)}, u32[]{:S(2)}) copy-start(s32[2]{0:T(128)} %param.13) | copy-start | bytes 28
  442.1 91.4 %copy-start.27 = (pred[32]{0:T(512)(128)(4,1)S(1)}, pred[32]{0:T(512)(128)(4,1)}, u32[]{:S(2)}) copy-start(pred[32]{0:T(512)(128)(4,1)} %constant.146) | copy-start | bytes 100
  442.1 91.4 %copy-start.28 = (pred[32]{0:T(512)(128)(4,1)S(1)}, pred[32]{0:T(512)(128)(4,1)}, u32[]{:S(2)}) copy-start(pred[32]{0:T(512)(128)(4,1)} %constant.145) | copy-start | bytes 100
  442.1 91.4 %copy-start.29 = (pred[32]{0:T(512)(128)(4,1)S(1)}, pred[32]{0:T(512)(128)(4,1)}, u32[]{:S(2)}) copy-start(pred[32]{0:T(512)(128)(4,1)} %constant.144) | copy-start | bytes 100
  442.1 96.3 %copy-start.19 = (pred[40]{0:T(512)(128)(4,1)S(1)}, pred[40]{0:T(512)(128)(4,1)}, u32[]{:S(2)}) copy-start(pred[40]{0:T(512)(128)(4,1)} %constant.169) | copy-start | bytes 124
  442.1 96.3 %copy-start.20 = (pred[40]{0:T(512)(128)(4,1)S(1)}, pred[40]{0:T(512)(128)(4,1)}, u32[]{:S(2)}) copy-start(pred[40]{0:T(512)(128)(4,1)} %constant.168) | copy-start | bytes 124
  442.2 96.3 %copy-start.21 = (pred[40]{0:T(512)(128)(4,1)S(1)}, pred[40]{0:T(512)(128)(4,1)}, u32[]{:S(2)}) copy-start(pred[40]{0:T(512)(128)(4,1)} %constant.167) | copy-start | bytes 124
  442.2 96.3 %copy-start.22 = (pred[40]{0:T(512)(128)(4,1)S(1)}, pred[40]{0:T(512)(128)(4,1)}, u32[]{:S(2)}) copy-start(pred[40]{0:T(512)(128)(4,1)} %constant.166) | copy-start | bytes 124
  442.2 96.3 %copy-start.23 = (pred[40]{0:T(512)(128)(4,1)S(1)}, pred[40]{0:T(512)(128)(4,1)}, u32[]{:S(2)}) copy-start(pred[40]{0:T(512)(128)(4,1)} %constant.165) | copy-start | bytes 124
  442.2 96.3 %copy-start.24 = (pred[40]{0:T(512)(128)(4,1)S(1)}, pred[40]{0:T(512)(128)(4,1)}, u32[]{:S(2)}) copy-start(pred[40]{0:T(512)(128)(4,1)} %constant.164) | copy-start | bytes 124
  442.2 96.3 %copy-start.25 = (pred[40]{0:T(512)(128)(4,1)S(1)}, pred[40]{0:T(512)(128)(4,1)}, u32[]{:S(2)}) copy-start(pred[40]{0:T(512)(128)(4,1)} %constant.163) | copy-start | bytes 124
  442.2 96.3 %copy-start.26 = (pred[40]{0:T(512)(128)(4,1)S(1)}, pred[40]{0:T(512)(128)(4,1)}, u32[]{:S(2)}) copy-start(pred[40]{0:T(512)(128)(4,1)} %constant.92.clone) | copy-start | bytes 124
  442.2 101.4 %copy-start.11 = (pred[40]{0:T(512)(128)(4,1)S(1)}, pred[40]{0:T(512)(128)(4,1)}, u32[]{:S(2)}) copy-start(pred[40]{0:T(512)(128)(4,1)} %constant.160) | copy-start | bytes 124
  442.2 101.4 %copy-start.12 = (pred[40]{0:T(512)(128)(4,1)S(1)}, pred[40]{0:T(512)(128)(4,1)}, u32[]{:S(2)}) copy-start(pred[40]{0:T(512)(128)(4,1)} %constant.159) | copy-start | bytes 124
  442.3 101.4 %copy-start.13 = (pred[40]{0:T(512)(128)(4,1)S(1)}, pred[40]{0:T(512)(128)(4,1)}, u32[]{:S(2)}) copy-start(pred[40]{0:T(512)(128)(4,1)} %constant.158) | copy-start | bytes 124
  442.3 101.3 %copy-start.14 = (pred[40]{0:T(512)(128)(4,1)S(1)}, pred[40]{0:T(512)(128)(4,1)}, u32[]{:S(2)}) copy-start(pred[40]{0:T(512)(128)(4,1)} %constant.157) | copy-start | bytes 124
  442.3 101.3 %copy-start.15 = (pred[40]{0:T(512)(128)(4,1)S(1)}, pred[40]{0:T(512)(128)(4,1)}, u32[]{:S(2)}) copy-start(pred[40]{0:T(512)(128)(4,1)} %constant.156) | copy-start | bytes 124
  442.3 101.3 %copy-start.16 = (pred[40]{0:T(512)(128)(4,1)S(1)}, pred[40]{0:T(512)(128)(4,1)}, u32[]{:S(2)}) copy-start(pred[40]{0:T(512)(128)(4,1)} %constant.155) | copy-start | bytes 124
  442.3 101.3 %copy-start.17 = (pred[40]{0:T(512)(128)(4,1)S(1)}, pred[40]{0:T(512)(128)(4,1)}, u32[]{:S(2)}) copy-start(pred[40]{0:T(512)(128)(4,1)} %constant.154) | copy-start | bytes 124
  442.3 101.3 %copy-start.18 = (pred[40]{0:T(512)(128)(4,1)S(1)}, pred[40]{0:T(512)(128)(4,1)}, u32[]{:S(2)}) copy-start(pred[40]{0:T(512)(128)(4,1)} %constant.91.clone) | copy-start | bytes 124
  475.7 109.2 %all-to-all-start.3 = ((f32[16,8,5,8,128]{4,3,2,1,0:T(8,128)}), f32[16,8,5,8,128]{4,3,2,1,0:T(8,128)}, u32[]{:S(2)}, u32[]{:S(2)}) async-start(f32[16,8,5,8,128]{4,3,2,1,0:T(8,128)} %copy.83), calls=%async_computation.3 | async-start | bytes 5242880 | tf_op jit(solution)/shard_map/all_to_all | solution.py:260
  (12 other events, 160.0 us)

commit v3 on v2

--- a/solution.py
+++ b/solution.py
@@ -181,7 +181,7 @@
     lax.fori_loop(0, groups, group_step, 0)
 
 
-def inverse_kernel(mutual, firsts, seconds, scale_one, scale_two, field, orbs, others, *rest):
+def inverse_kernel(true_pairs, firsts, seconds, weights, field, orbs, others, *rest):
     *base, left, place_high, place_low, out = rest
     planes = orbs.shape[1]
     count = left.shape[1] // 3
@@ -221,9 +221,14 @@
                     slot = group * pack + 2 * couple + member
                     one, two = firsts[slot], seconds[slot]
                     potential = solved[:, member * points : (member + 1) * points]
-                    out[one, plane] += potential * others[two, plane] * scale_one[slot]
-                    if mutual:
-                        out[two, plane] += potential * orbs[one, plane] * scale_two[slot]
+                    scale = weights[two]
+                    if not base:
+                        real = slot < true_pairs
+                        scale = jnp.where(real, scale, 0.0)
+                        twin = jnp.where(real & (one != two), weights[one], 0.0)
+                    out[one, plane] += potential * others[two, plane] * scale
+                    if not base:
+                        out[two, plane] += potential * orbs[one, plane] * twin
         return 0
 
     lax.fori_loop(0, groups, group_step, 0)
@@ -261,10 +266,6 @@
             value, both, split_axis=0, concat_axis=0, tiled=True, axis_index_groups=all_sides
         )
 
-    visiting = [passed_along(orbitals[k : k + 1], "band", half) for k in range(local)]
-    mine = to_planes(orbitals)
-    visiting = [to_planes(value) for value in visiting]
-
     catalog = jnp.arange(occupations.shape[0], dtype=jnp.int32)
     own_weight = jnp.sum(
         jnp.where(slot_ids[:, None] == catalog[None, :], occupations[None, :], 0.0), axis=1
@@ -273,6 +274,23 @@
     upper = band >= half
     my_weights = jnp.where(upper, weights[1], weights[0])
     other_weights = jnp.where(upper, weights[0], weights[1]).reshape(half, local)
+
+    orbitals, my_weights, other_weights = lax.optimization_barrier(
+        (orbitals, my_weights, other_weights)
+    )
+    def beside(part, value, work):
+        part, value = lax.optimization_barrier((part, value))
+        return lax.optimization_barrier((passed_along(part, "band", half), work(value)))
+
+    def parts_of(index):
+        cuts = [step * orbitals.shape[1] // 3 for step in range(4)]
+        return [
+            orbitals[index : index + 1, low:high] for low, high in zip(cuts[:-1], cuts[1:])
+        ]
+
+    parts = parts_of(0)
+    moved, mine = beside(parts[0], orbitals, to_planes)
+    arriving = [moved]
 
     second_high, second_low = split_table(sine_second)
     empty = jnp.zeros_like(second_low)
@@ -306,28 +324,31 @@
     smem = pl.BlockSpec(memory_space=pltpu.SMEM)
     params = pltpu.CompilerParams(vmem_limit_bytes=50 * 2**20)
 
-    def modal(coeffs):
-        share = coeffs.shape[2]
+    def modal(swapped):
+        shape = (devices, planes) + swapped.shape[2:]
+        share = shape[2]
         rounds = -(-share // per_group) + 1
         inner = lax.dynamic_slice_in_dim(
             jnp.tile(inner_tiles, (rounds, 1, 1)), lax.rem(device * share, per_group), share
         )
         both_squares = (squares[0][:, None] + inner.reshape(1, -1)).astype(jnp.float32)
         screen = 1.0 / (1.0 + both_squares / jnp.float32(points * points))
-        flat = exchanged(coeffs).reshape(points, share * ROWS * LANES)
+        flat = swapped.reshape(points, share * ROWS * LANES)
         spectral = screen * jnp.einsum(
             "xm,xa->am", flat, first_sent, precision=lax.Precision.HIGH
         )
         spatial = jnp.einsum("am,xa->xm", spectral, first_sent, precision=lax.Precision.HIGH)
-        return exchanged(spatial.reshape(coeffs.shape))
+        return exchanged(spatial.reshape(shape))
 
     def pair_cost(pairs):
         work = pairs * planes * points * points * 2 * LANES * 4
         return pl.CostEstimate(flops=work, bytes_accessed=2**24, transcendentals=0)
 
-    def fields_of(pairs, others):
-        tables = [jnp.asarray(np.array(part, np.int32)) for part in zip(*pairs)]
-        groups = len(pairs) // pack
+    def tables_of(pairs):
+        return [jnp.asarray(np.array(part, np.int32)) for part in zip(*pairs)]
+
+    def swapped_of(tables, others):
+        groups = tables[0].shape[0] // pack
         share = -(-groups * per_group // devices)
         coeffs = pl.pallas_call(
             forward_kernel,
@@ -335,37 +356,48 @@
             in_specs=[smem] * 2 + [vmem] * 5,
             out_specs=vmem,
             compiler_params=params,
-            cost_estimate=pair_cost(len(pairs)),
+            cost_estimate=pair_cost(tables[0].shape[0]),
         )(*tables, mine, others, forward_left, *forward_place)
-        return tables, modal(coeffs)
-
-    def terms_of(tables, field, others, scales, base):
+        return exchanged(coeffs)
+
+    def terms_of(true_pairs, tables, weights, field, others, base):
         extra = [] if base is None else [base]
         return pl.pallas_call(
-            functools.partial(inverse_kernel, base is None),
+            functools.partial(inverse_kernel, true_pairs),
             out_shape=jax.ShapeDtypeStruct(mine.shape, jnp.float32),
-            in_specs=[smem] * 4 + [vmem] * (6 + len(extra)),
+            in_specs=[smem] * 3 + [vmem] * (6 + len(extra)),
             out_specs=vmem,
             compiler_params=params,
             cost_estimate=pair_cost(tables[0].shape[0]),
-        )(*tables, *scales, field, mine, others, *extra, inverse_left, *inverse_place)
+        )(*tables, weights, field, mine, others, *extra, inverse_left, *inverse_place)
 
     pairs = [(i, j) for i in range(own) for j in range(i, own)]
     true_pairs = len(pairs)
     pairs += [(0, 0)] * (-true_pairs % pack)
-    valid = np.arange(len(pairs)) < true_pairs
-    apart = np.array([i != j for i, j in pairs])
-    tables, field = fields_of(pairs, mine)
-    scales = (
-        jnp.where(valid, my_weights[tables[1]], 0.0),
-        jnp.where(valid & apart, my_weights[tables[0]], 0.0),
-    )
+    tables = tables_of(pairs)
+    moved, swapped = beside(parts[1], mine, lambda value: swapped_of(tables, value))
+    arriving.append(moved)
+    moved, field = beside(parts[2], swapped, modal)
+    arriving.append(moved)
+    ready = [(true_pairs, tables, my_weights, field, mine)]
     cross = [(i, j) for i in range(own) for j in range(half)]
-    solved = [fields_of(cross, value) for value in visiting]
-    terms = terms_of(tables, field, mine, scales, None)
-    for k, (tables, field) in enumerate(solved):
-        scale = other_weights[:, k][tables[1]]
-        terms = terms_of(tables, field, visiting[k], (scale, scale), terms)
+    tables = tables_of(cross)
+    for k in range(local):
+        value = jnp.concatenate(arriving, axis=1)
+        parts = parts_of(k + 1) if k + 1 < local else [None] * 3
+        arriving = []
+        others = None
+        for part, work in zip(parts, (to_planes, lambda v: swapped_of(tables, v), modal)):
+            if part is None:
+                value = work(value)
+            else:
+                moved, value = beside(part, value, work)
+                arriving.append(moved)
+            others = value if others is None else others
+        ready.append((len(cross), tables, other_weights[:, k], value, others))
+    terms = None
+    for item in ready:
+        terms = terms_of(*item, terms)
     return lax.all_to_all(
         terms, "band", split_axis=0, concat_axis=1, tiled=True, axis_index_groups=sides
     )

time: 654 us -> 646 us (0.988)
  blocking collectives: 97 us -> 145 us
  waiting for transfers between devices: 341 us -> 297 us
  other arithmetic: 16.5 us -> 6.83 us
    all_to_all x6 -> x5, waiting for transfers between devices: 135 us -> 0.01 us  [exchanged(): lax.all_to_all(value, both, split_axis=0, concat_axis=0, tiled=True, axis...]
    all_to_all x0 -> x2, blocking collectives: none -> 69.6 us  [the longest x1 37.5 us: exchanged(): lax.all_to_all(value, both, split_axis=0, concat_axis=0, tiled=True, axis...]
    ppermute x2 -> x6, waiting for transfers between devices: 177 us -> 242 us  [passed_along(): return lax.ppermute(value, axis, pairs)]
    all_to_all x3 -> x2, waiting for transfers between devices: 29.2 us -> 54.7 us  [to_planes(): lax.all_to_all(value, 'band', split_axis=1, concat_axis=0, tiled=True, ax...]
    unnamed x1, blocking collectives: 47.9 us -> 23.1 us
    select_n x3 -> x1, other arithmetic: 10.3 us -> 0.08 us  [spread_form(): jnp.where(upper, weights[0], weights[1]).reshape(half, local)]
    all_to_all x3 -> x2, starting transfers between devices: 13.2 us -> 9.34 us  [to_planes(): lax.all_to_all(value, 'band', split_axis=1, concat_axis=0, tiled=True, ax...]
    all_to_all x6 -> x5, starting transfers between devices: 30.5 us -> 29.8 us  [exchanged(): lax.all_to_all(value, both, split_axis=0, concat_axis=0, tiled=True, axis...]
  transfers between devices with their start and end apart: 11 -> 13, of which waited for: 10 -> 7; matrix products, arithmetic and copies ran while one was open for 10% -> 2% of each run, Pallas kernels for 11% -> 6%
where the time goes in v3:
time: 646 us; the launch traced here: 644 us
  waiting for transfers between devices  297 us (46%)
  blocking collectives  145 us (22%)
  Pallas kernels  91.2 us (14%)
  starting transfers between devices  46.9 us (7%)
  local copies, waits for them, and re-layouts  42.4 us (7%)
  matrix products  13.7 us (2%)
  other arithmetic  6.83 us (1%)
    ppermute x6, waiting for transfers between devices, passed_along(): return lax.ppermute(value, axis, pairs)  242 us
    all_to_all x2, waiting for transfers between devices, to_planes(): lax.all_to_all(value, 'band', split_axis=1, concat_axis=0, tiled=True, ax...  54.7 us
    pallas_call x3, Pallas kernels, terms_of(): pl.pallas_call(functools.partial(inverse_kernel, true_pairs), out_shape=j...  52.8 us
    all_to_all x1, blocking collectives, spread_form(): lax.all_to_all(terms, 'band', split_axis=0, concat_axis=1, tiled=True, ax...  52.1 us
    pallas_call x3, Pallas kernels, swapped_of(): pl.pallas_call(forward_kernel, out_shape=jax.ShapeDtypeStruct((devices, p...  38.4 us
    all_to_all x1, blocking collectives, exchanged(): lax.all_to_all(value, both, split_axis=0, concat_axis=0, tiled=True, axis...  37.5 us
    all_to_all x1, blocking collectives, to_planes(): lax.all_to_all(value, 'band', split_axis=1, concat_axis=0, tiled=True, ax...  32.1 us
    all_to_all x5, starting transfers between devices, exchanged(): lax.all_to_all(value, both, split_axis=0, concat_axis=0, tiled=True, axis...  29.8 us
  transfers between devices with their start and end apart: 13, of which 7 were waited for; matrix products, arithmetic and copies ran while one was open for 2% of the time, Pallas kernels for 6%

profile of v3, /device:TPU:0, one launch (start us, length us, event | category | flops | bytes accessed | tf_op | source)
XLA Modules:
  0.0 644.0 jit_solution(3490447493497163707)
XLA Ops:
  3.0 23.1 %all-reduce.5 = f32[16]{0:T(128)S(1)} all-reduce(f32[16]{0:T(128)S(1)} %dynamic-update-slice), channel_id=1, replica_groups=mesh['band'=8,'slab'=4] {'band'}, use_global_device_ids=true, to_apply=%add.5 | all-reduce | flops 16 | bytes 128
  28.5 4.7 copy.77
  33.2 5.0 all-to-all-start
  40.2 3.4 fusion.98
  43.6 52.6 %all-to-all-done = f32[2,32,128,128]{3,2,0,1:T(8,128)} async-done(((f32[2,32,128,128]{3,2,0,1:T(8,128)}), f32[2,32,128,128]{3,2,0,1:T(8,128)}, u32[]{:S(2)}, u32[]{:S(2)}) %all-to-all-start) | async-done | bytes 4194336 | tf_op jit(solution)/shard_map/all_to_all | solution.py:260
  96.2 4.7 copy.78
  100.9 14.6 %shard_map.82 = f32[16,8,6,8,128]{4,3,2,1,0:T(8,128)} custom-call(s32[40]{0:T(128)S(1)} %copy-done.11, s32[40]{0:T(128)S(1)} %copy-done.10, f32[8,8,128,128]{3,2,1,0:T(8,128)} %bitcast.94, f32[8,8,128,128]{3,2,1,0:T(8,128)} %bitcast.95, bf16[96,256]{1,0:T(8,128)(2,1)S(1)} %copy.81.left, bf16[4,256,256]{2,1,0:T(8,128)(2,1)S(1)} %copy.82.place_high, ...), custom_call_target="tpu_custom_call" | custom-call | flops 5368709120 | bytes 16777216 | tf_op jit(solution)/shard_map/pallas_call | solution.py:353
  115.6 4.5 all-to-all-start.1
  121.1 56.1 %collective-permute-done.1 = f32[1,11,128,128]{3,2,0,1:T(8,128)S(1)} collective-permute-done((f32[1,11,128,128]{3,2,0,1:T(8,128)}, f32[1,11,128,128]{3,2,0,1:T(8,128)S(1)}, u32[]{:S(2)}, u32[]{:S(2)}) %collective-permute-start.1) | collective-permute-done | bytes 720928 | tf_op jit(solution)/shard_map/ppermute | solution.py:19
  177.3 4.3 reshape.172
  181.5 3.2 fusion
  188.9 7.4 %all-to-all-start.2 = ((f32[16,8,6,8,128]{4,3,2,1,0:T(8,128)}), f32[16,8,6,8,128]{4,3,2,1,0:T(8,128)}, u32[]{:S(2)}, u32[]{:S(2)}) async-start(f32[16,8,6,8,128]{4,3,2,1,0:T(8,128)} %copy.86), calls=%async_computation.2 | async-start | bytes 6291456 | tf_op jit(solution)/shard_map/all_to_all | solution.py:265
  196.8 58.0 %collective-permute-done.2 = f32[1,11,128,128]{3,2,0,1:T(8,128)} collective-permute-done((f32[1,11,128,128]{3,2,0,1:T(8,128)S(1)}, f32[1,11,128,128]{3,2,0,1:T(8,128)}, u32[]{:S(2)}, u32[]{:S(2)}) %collective-permute-start.2) | collective-permute-done | bytes 720928 | tf_op jit(solution)/shard_map/ppermute | solution.py:19
  254.8 3.0 pad_maximum_fusion
  257.8 4.4 all-to-all-start.3
  262.1 2.9 collective-permute-start.3
  265.1 33.7 %collective-permute-done.3 = f32[1,10,128,128]{3,2,0,1:T(8,128)} collective-permute-done((f32[1,10,128,128]{3,2,0,1:T(8,128)}, f32[1,10,128,128]{3,2,0,1:T(8,128)}, u32[]{:S(2)}, u32[]{:S(2)}) %collective-permute-start.3) | collective-permute-done | bytes 655392 | tf_op jit(solution)/shard_map/ppermute | solution.py:19
  302.9 11.7 %shard_map.83 = f32[16,8,5,8,128]{4,3,2,1,0:T(8,128)} custom-call(s32[32]{0:T(128)S(1)} %copy-done.9, s32[32]{0:T(128)S(1)} %copy-done.8, f32[8,8,128,128]{3,2,1,0:T(8,128)} %bitcast.96, f32[4,8,128,128]{3,2,1,0:T(8,128)S(1)} %bitcast.90, bf16[96,256]{1,0:T(8,128)(2,1)S(1)} %copy.81.left, bf16[4,256,256]{2,1,0:T(8,128)(2,1)S(1)} %copy-done.3, ...), custom_call_target="tpu_custom_call" | custom-call | flops 4294967296 | bytes 16777216 | tf_op jit(solution)/shard_map/pallas_call | solution.py:353
  314.6 5.9 all-to-all-start.4
  322.6 47.2 %collective-permute-done.4 = f32[1,11,128,128]{3,2,0,1:T(8,128)} collective-permute-done((f32[1,11,128,128]{3,2,0,1:T(8,128)}, f32[1,11,128,128]{3,2,0,1:T(8,128)}, u32[]{:S(2)}, u32[]{:S(2)}) %collective-permute-start.4) | collective-permute-done | bytes 720928 | tf_op jit(solution)/shard_map/ppermute | solution.py:19
  369.9 3.5 reshape.173
  379.9 7.2 %all-to-all-start.5 = ((f32[16,8,5,8,128]{4,3,2,1,0:T(8,128)}), f32[16,8,5,8,128]{4,3,2,1,0:T(8,128)}, u32[]{:S(2)}, u32[]{:S(2)}) async-start(f32[16,8,5,8,128]{4,3,2,1,0:T(8,128)} %copy.93), calls=%async_computation.5 | async-start | bytes 5242880 | tf_op jit(solution)/shard_map/all_to_all | solution.py:265
  389.3 47.3 %collective-permute-done.5 = f32[1,11,128,128]{3,2,0,1:T(8,128)} collective-permute-done((f32[1,11,128,128]{3,2,0,1:T(8,128)}, f32[1,11,128,128]{3,2,0,1:T(8,128)}, u32[]{:S(2)}, u32[]{:S(2)}) %collective-permute-start.5) | collective-permute-done | bytes 720928 | tf_op jit(solution)/shard_map/ppermute | solution.py:19
  438.3 32.1 %all_to_all.90 = f32[1,32,128,128]{3,2,0,1:T(8,128)S(1)} all-to-all(f32[1,32,128,128]{3,2,0,1:T(8,128)S(1)} %pad_maximum_fusion.1), channel_id=1, replica_groups={{0,4,8,12},{16,20,24,28},{1,5,9,13},{17,21,25,29},{2,6,10,14},{18,22,26..., dimensions={1} | all-to-all | bytes 4194304 | tf_op jit(solution)/shard_map/all_to_all | solution.py:260
  470.5 12.1 %shard_map.84 = f32[16,8,5,8,128]{4,3,2,1,0:T(8,128)} custom-call(s32[32]{0:T(128)S(1)} %copy-done.9, s32[32]{0:T(128)S(1)} %copy-done.8, f32[8,8,128,128]{3,2,1,0:T(8,128)} %bitcast.97, f32[4,8,128,128]{3,2,1,0:T(8,128)S(1)} %bitcast.92, bf16[96,256]{1,0:T(8,128)(2,1)S(1)} %copy.81.left, bf16[4,256,256]{2,1,0:T(8,128)(2,1)S(1)} %copy-done.4, ...), custom_call_target="tpu_custom_call" | custom-call | flops 4294967296 | bytes 16777216 | tf_op jit(solution)/shard_map/pallas_call | solution.py:353
  482.6 37.5 %all_to_all.91 = f32[16,8,5,8,128]{4,3,2,1,0:T(8,128)} all-to-all(f32[16,8,5,8,128]{4,3,2,1,0:T(8,128)} %shard_map.84), channel_id=1, replica_groups={{0,1,2,3,4,5,6,7,8,9,10,11,12,13,14,15},{16,17,18,19,20,21,22,23,24,25,..., dimensions={0} | all-to-all | bytes 5242880 | tf_op jit(solution)/shard_map/all_to_all | solution.py:265
  520.1 3.5 reshape.174
  530.1 4.8 all-to-all-start.8
  535.2 20.4 %shard_map.85.rest_0_ = f32[8,8,128,128]{3,2,1,0:T(8,128)} custom-call(s32[40]{0:T(128)S(1)} %copy-done.11, s32[40]{0:T(128)S(1)} %copy-done.10, f32[8]{0:T(128)S(1)} %get-tuple-element.57.weights, f32[16,8,6,8,128]{4,3,2,1,0:T(8,128)} %all-to-all-done.2.field, f32[8,8,128,128]{3,2,1,0:T(8,128)} %bitcast.98, f32[8,8,128,128]{3,2,1,0:T(8,128)} %bitcast.99, ...), custom_call_target="tpu_custom_call" | custom-call | flops 5368709120 | bytes 16777216 | tf_op jit(solution)/shard_map/pallas_call | solution.py:365
  555.6 16.2 %shard_map.86.rest_0_ = f32[8,8,128,128]{3,2,1,0:T(8,128)} custom-call(s32[32]{0:T(128)S(1)} %copy-done.9, s32[32]{0:T(128)S(1)} %copy-done.8, f32[4]{0:T(128)S(1)} %get-tuple-element.59.weights, f32[16,8,5,8,128]{4,3,2,1,0:T(8,128)} %all-to-all-done.5.field, f32[8,8,128,128]{3,2,1,0:T(8,128)} %bitcast.100, f32[4,8,128,128]{3,2,1,0:T(8,128)S(1)} %bitcast.91, ...), custom_call_target="tpu_custom_call" | custom-call | flops 4294967296 | bytes 16777216 | tf_op jit(solution)/shard_map/pallas_call | solution.py:365
  573.4 16.2 %shard_map.87 = f32[8,8,128,128]{3,2,1,0:T(8,128)} custom-call(s32[32]{0:T(128)S(1)} %copy-done.9, s32[32]{0:T(128)S(1)} %copy-done.8, f32[4]{0:T(128)S(1)} %get-tuple-element.60.weights, f32[16,8,5,8,128]{4,3,2,1,0:T(8,128)} %all-to-all-done.8.field, f32[8,8,128,128]{3,2,1,0:T(8,128)} %bitcast.101, f32[4,8,128,128]{3,2,1,0:T(8,128)S(1)} %bitcast.93, ...), custom_call_target="tpu_custom_call" | custom-call | flops 4294967296 | bytes 16777216 | tf_op jit(solution)/shard_map/pallas_call | solution.py:365
  589.6 52.1 %all_to_all.92 = f32[8,8,128,128]{3,2,1,0:T(8,128)S(1)} all-to-all(f32[8,8,128,128]{3,2,1,0:T(8,128)} %shard_map.87), channel_id=1, replica_groups={{0,4,8,12},{16,20,24,28},{1,5,9,13},{17,21,25,29},{2,6,10,14},{18,22,26..., dimensions={0} | all-to-all | bytes 8388608 | tf_op jit(solution)/shard_map/all_to_all | solution.py:401
  (101 shorter events, 39.6 us)
Async XLA Ops:
  33.2 5.1 copy-start.16
  33.2 63.0 %all-to-all-start = ((f32[2,32,128,128]{3,2,0,1:T(8,128)}), f32[2,32,128,128]{3,2,0,1:T(8,128)}, u32[]{:S(2)}, u32[]{:S(2)}) async-start(f32[2,32,128,128]{3,2,0,1:T(8,128)} %copy.77), calls=%async_computation | async-start | bytes 8388608 | tf_op jit(solution)/shard_map/all_to_all | solution.py:260
  38.2 62.7 %collective-permute-start = (f32[1,10,128,128]{3,2,0,1:T(8,128)S(1)}, f32[1,10,128,128]{3,2,0,1:T(8,128)}, u32[]{:S(2)}, u32[]{:S(2)}) collective-permute-start(f32[1,10,128,128]{3,2,0,1:T(8,128)S(1)} %get-tuple-element.34), channel_id=1, source_target_pairs={{0,16},{4,20},{8,24},{12,28},{16,0},{20,4},{24,8},{28,12},{1,17},{... | collective-permute-start | bytes 1966088 | tf_op jit(solution)/shard_map/ppermute | solution.py:19
  38.9 0.6 copy-start.12
  38.9 0.6 copy-start.14
  40.0 60.9 %copy-start.2 = (bf16[4,256,256]{2,1,0:T(8,128)(2,1)}, bf16[4,256,256]{2,1,0:T(8,128)(2,1)S(1)}, u32[]{:S(2)}) copy-start(bf16[4,256,256]{2,1,0:T(8,128)(2,1)S(1)} %copy.82.place_high) | copy-start | bytes 1572868
  40.2 60.7 %copy-start.5 = (bf16[4,256,256]{2,1,0:T(8,128)(2,1)}, bf16[4,256,256]{2,1,0:T(8,128)(2,1)S(1)}, u32[]{:S(2)}) copy-start(bf16[4,256,256]{2,1,0:T(8,128)(2,1)S(1)} %copy.83.place_low) | copy-start | bytes 1572868
  96.2 4.7 copy-start.10
  96.2 4.8 copy-start.11
  115.6 61.7 %all-to-all-start.1 = ((f32[16,8,6,8,128]{4,3,2,1,0:T(8,128)}), f32[16,8,6,8,128]{4,3,2,1,0:T(8,128)}, u32[]{:S(2)}, u32[]{:S(2)}) async-start(f32[16,8,6,8,128]{4,3,2,1,0:T(8,128)} %shard_map.82), calls=%async_computation.1 | async-start | bytes 6291456 | tf_op jit(solution)/shard_map/all_to_all | solution.py:265
  120.1 57.2 %collective-permute-start.1 = (f32[1,11,128,128]{3,2,0,1:T(8,128)}, f32[1,11,128,128]{3,2,0,1:T(8,128)S(1)}, u32[]{:S(2)}, u32[]{:S(2)}) collective-permute-start(f32[1,11,128,128]{3,2,0,1:T(8,128)} %get-tuple-element.38), channel_id=1, source_target_pairs={{0,16},{4,20},{8,24},{12,28},{16,0},{20,4},{24,8},{28,12},{1,17},{... | collective-permute-start | bytes 2162696 | tf_op jit(solution)/shard_map/ppermute | solution.py:19
  188.9 65.9 %all-to-all-start.2 = ((f32[16,8,6,8,128]{4,3,2,1,0:T(8,128)}), f32[16,8,6,8,128]{4,3,2,1,0:T(8,128)}, u32[]{:S(2)}, u32[]{:S(2)}) async-start(f32[16,8,6,8,128]{4,3,2,1,0:T(8,128)} %copy.86), calls=%async_computation.2 | async-start | bytes 6291456 | tf_op jit(solution)/shard_map/all_to_all | solution.py:265
  196.3 58.5 %collective-permute-start.2 = (f32[1,11,128,128]{3,2,0,1:T(8,128)S(1)}, f32[1,11,128,128]{3,2,0,1:T(8,128)}, u32[]{:S(2)}, u32[]{:S(2)}) collective-permute-start(f32[1,11,128,128]{3,2,0,1:T(8,128)S(1)} %get-tuple-element.42), channel_id=1, source_target_pairs={{0,16},{4,20},{8,24},{12,28},{16,0},{20,4},{24,8},{28,12},{1,17},{... | collective-permute-start | bytes 2162696 | tf_op jit(solution)/shard_map/ppermute | solution.py:19
  257.8 43.1 %copy-start.8 = (s32[32]{0:T(128)S(1)}, s32[32]{0:T(128)}, u32[]{:S(2)}) copy-start(s32[32]{0:T(128)} %constant.84.clone.seconds) | copy-start | bytes 388
  257.8 43.1 %copy-start.9 = (s32[32]{0:T(128)S(1)}, s32[32]{0:T(128)}, u32[]{:S(2)}) copy-start(s32[32]{0:T(128)} %constant.83.clone.firsts) | copy-start | bytes 388
  257.8 43.1 %all-to-all-start.3 = ((f32[1,32,128,128]{3,2,0,1:T(8,128)}), f32[1,32,128,128]{3,2,0,1:T(8,128)S(1)}, u32[]{:S(2)}, u32[]{:S(2)}) async-start(f32[1,32,128,128]{3,2,0,1:T(8,128)} %pad_maximum_fusion), calls=%async_computation.3 | async-start | bytes 4194304 | tf_op jit(solution)/shard_map/all_to_all | solution.py:260
  262.1 36.6 %collective-permute-start.3 = (f32[1,10,128,128]{3,2,0,1:T(8,128)}, f32[1,10,128,128]{3,2,0,1:T(8,128)}, u32[]{:S(2)}, u32[]{:S(2)}) collective-permute-start(f32[1,10,128,128]{3,2,0,1:T(8,128)} %get-tuple-element.45), channel_id=1, source_target_pairs={{0,16},{4,20},{8,24},{12,28},{16,0},{20,4},{24,8},{28,12},{1,17},{... | collective-permute-start | bytes 1966088 | tf_op jit(solution)/shard_map/ppermute | solution.py:19
  300.9 1.0 copy-start.3
  301.9 1.0 copy-start.6
  314.6 55.2 %all-to-all-start.4 = ((f32[16,8,5,8,128]{4,3,2,1,0:T(8,128)}), f32[16,8,5,8,128]{4,3,2,1,0:T(8,128)}, u32[]{:S(2)}, u32[]{:S(2)}) async-start(f32[16,8,5,8,128]{4,3,2,1,0:T(8,128)} %shard_map.83), calls=%async_computation.4 | async-start | bytes 5242880 | tf_op jit(solution)/shard_map/all_to_all | solution.py:265
  320.5 49.4 %collective-permute-start.4 = (f32[1,11,128,128]{3,2,0,1:T(8,128)}, f32[1,11,128,128]{3,2,0,1:T(8,128)}, u32[]{:S(2)}, u32[]{:S(2)}) collective-permute-start(f32[1,11,128,128]{3,2,0,1:T(8,128)} %get-tuple-element.49), channel_id=1, source_target_pairs={{0,16},{4,20},{8,24},{12,28},{16,0},{20,4},{24,8},{28,12},{1,17},{... | collective-permute-start | bytes 2162696 | tf_op jit(solution)/shard_map/ppermute | solution.py:19
  379.9 56.6 %all-to-all-start.5 = ((f32[16,8,5,8,128]{4,3,2,1,0:T(8,128)}), f32[16,8,5,8,128]{4,3,2,1,0:T(8,128)}, u32[]{:S(2)}, u32[]{:S(2)}) async-start(f32[16,8,5,8,128]{4,3,2,1,0:T(8,128)} %copy.93), calls=%async_computation.5 | async-start | bytes 5242880 | tf_op jit(solution)/shard_map/all_to_all | solution.py:265
  387.2 49.4 %collective-permute-start.5 = (f32[1,11,128,128]{3,2,0,1:T(8,128)}, f32[1,11,128,128]{3,2,0,1:T(8,128)}, u32[]{:S(2)}, u32[]{:S(2)}) collective-permute-start(f32[1,11,128,128]{3,2,0,1:T(8,128)} %get-tuple-element.53), channel_id=1, source_target_pairs={{0,16},{4,20},{8,24},{12,28},{16,0},{20,4},{24,8},{28,12},{1,17},{... | collective-permute-start | bytes 2162696 | tf_op jit(solution)/shard_map/ppermute | solution.py:19
  438.3 32.2 %copy-start.4 = (bf16[4,256,256]{2,1,0:T(8,128)(2,1)S(1)}, bf16[4,256,256]{2,1,0:T(8,128)(2,1)}, u32[]{:S(2)}) copy-start(bf16[4,256,256]{2,1,0:T(8,128)(2,1)} %copy-done.2) | copy-start | bytes 1572868
  438.3 32.1 %copy-start.7 = (bf16[4,256,256]{2,1,0:T(8,128)(2,1)S(1)}, bf16[4,256,256]{2,1,0:T(8,128)(2,1)}, u32[]{:S(2)}) copy-start(bf16[4,256,256]{2,1,0:T(8,128)(2,1)} %copy-done.5) | copy-start | bytes 1572868
  470.5 12.1 %copy-start = (f32[1,32,128,128]{3,2,0,1:T(8,128)}, f32[1,32,128,128]{3,2,0,1:T(8,128)S(1)}, u32[]{:S(2)}) copy-start(f32[1,32,128,128]{3,2,0,1:T(8,128)S(1)} %all_to_all.90) | copy-start | bytes 6291460
  530.1 5.0 copy-start.13
  530.1 5.0 copy-start.15
  530.1 41.7 %all-to-all-start.8 = ((f32[16,8,5,8,128]{4,3,2,1,0:T(8,128)}), f32[16,8,5,8,128]{4,3,2,1,0:T(8,128)}, u32[]{:S(2)}, u32[]{:S(2)}) async-start(f32[16,8,5,8,128]{4,3,2,1,0:T(8,128)} %copy.98), calls=%async_computation.8 | async-start | bytes 5242880 | tf_op jit(solution)/shard_map/all_to_all | solution.py:265
  571.8 1.6 copy-start.1
